TPU v7x, 128 devices: a whole 4x4x4 slice. The times are simulated.
128 devices in a mesh: dp: 16 (over y, x), tensor: 8 (over z, core).
Axes of the slice: x: 4, y: 4, z: 4, core: 2. Of those that a mesh axis runs over, the one named last changes fastest.
Arguments:
- hidden_acts: bfloat16 [16384, 12800], P('dp', 'tensor'), may hold values from -6 to 6
- out_grads: bfloat16 [16384, 2560], P(('dp', 'tensor')), may hold values from -0.1875 to 0.1875
- error: bfloat16 [16, 12800, 2560], P('dp', 'tensor'), may hold values from -6 to 6
- basis: bfloat16 [2560, 64], replicated, may hold values from -0.125 to 0.125
Outputs:
- update: bfloat16 [12800, 2560], P('tensor', 'dp')
- new_error: bfloat16 [16, 12800, 2560], P('dp', 'tensor')
All inputs are finite; a program needn't handle non-finite values.
Results may differ from a plain program's by a relative error of at most 0.013.
Values may be sent and summed in bfloat16 or wider, within the bound.
A program may use at most 128 MiB of HBM per device.

v0:
```python
import jax
import jax.numpy as jnp
from jax import lax
from jax.sharding import PartitionSpec as P


def orthonormal(left_rows, gram):
    lower = jnp.linalg.cholesky(gram)
    solved = jax.scipy.linalg.solve_triangular(lower, left_rows.T, lower=True)
    return solved.T.astype(jnp.bfloat16)


def shards(hidden_acts, out_grads, error, basis):
    breadth = out_grads.shape[1]
    grad = lax.dot_general(
        hidden_acts,
        lax.all_gather(out_grads, "tensor", axis=0, tiled=True),
        (((0,), (0,)), ((), ())),
        preferred_element_type=jnp.float32,
    )
    merged = (grad + error[0].astype(jnp.float32)).astype(jnp.bfloat16)
    p_local = jnp.dot(merged, basis, preferred_element_type=jnp.float32)
    p_total = lax.psum(p_local, "dp")
    gram = lax.psum(jnp.dot(p_total.T, p_total, precision=lax.Precision.HIGHEST), "tensor")
    p_hat = orthonormal(p_total, gram)
    q_term = lax.dot_general(
        merged, p_hat, (((0,), (0,)), ((), ())), preferred_element_type=jnp.float32
    )
    q_total = lax.psum(q_term, ("dp", "tensor"))
    full = jnp.dot(
        p_hat.astype(jnp.float32), q_total.T, precision=lax.Precision.HIGHEST
    ) / lax.axis_size("dp")
    new_error = (merged.astype(jnp.float32) - full).astype(jnp.bfloat16)[None]
    own_columns = breadth // lax.axis_size("dp")
    update = lax.dynamic_slice_in_dim(
        full, lax.axis_index("dp") * own_columns, own_columns, 1
    ).astype(jnp.bfloat16)
    return (update, new_error)


def solution(mesh):
    placed = (P("dp", "tensor"), P(("dp", "tensor"), None), P("dp", "tensor", None), P())
    return jax.shard_map(
        shards,
        mesh=mesh,
        in_specs=placed,
        out_specs=(P("tensor", "dp"), P("dp", "tensor", None)),
        check_vma=False,
    )
```

profile of v0, /device:TPU:0, one launch (start us, length us, event | category | flops | bytes accessed | tf_op | source)
XLA Modules:
  0.0 369.2 jit_solution(725019417703440955)
XLA Ops:
  7.2 0.0 copy-start
  7.2 0.0 all-gather.2.cloned.1.call-start
  7.2 0.7 all-gather.2.cloned.1.call-update
  7.9 0.0 all-reduce.3.cloned.1.call-start
  8.0 41.0 %all-gather.2.cloned.1.call-done = bf16[1024,2560]{1,0:T(8,128)(2,1)} async-done(((bf16[128,2560]{1,0:T(8,128)(2,1)}), bf16[1024,2560]{1,0:T(8,128)(2,1)}) %all-gather.2.cloned.1.call-update) | async-done | bytes 5242896 | tf_op jit(solution)/shard_map/all_gather | solution.py:17
  48.9 0.0 copy-done
  48.9 0.0 copy-start.2
  48.9 12.4 %fusion = bf16[1600,2560]{1,0:T(8,128)(2,1)S(1)} fusion(bf16[1024,1600]{0,1:T(8,128)(2,1)S(1)} %copy-done, bf16[1024,2560]{1,0:T(8,128)(2,1)} %all-gather.2.cloned.1.call-done, bf16[1,1600,2560]{2,1,0:T(8,128)(2,1)} %param.6), kind=kOutput, calls=%fused_computation.1 | convolution fusion | flops 8400896000 | bytes 24903680 | tf_op jit(solution)/shard_map/dot_general | solution.py:15
  61.4 0.0 copy-start.1
  61.4 3.3 copy-done.1
  64.7 0.0 copy-done.2
  64.7 3.3 fusion.5
  68.0 0.0 all-reduce.3.cloned.1.call-update
  68.0 0.0 all-reduce.5.cloned.1.call-start
  68.1 84.1 %all-reduce.3.cloned.1.call-done = f32[1600,64]{0,1:T(8,128)} async-done(((f32[1600,64]{0,1:T(8,128)}), f32[1600,64]{0,1:T(8,128)}) %all-reduce.3.cloned.1.call-update) | async-done | bytes 409616 | tf_op jit(solution)/shard_map/psum | solution.py:23
  152.2 1.7 fusion.6
  153.9 24.6 %psum.22 = f32[64,64]{0,1:T(8,128)S(1)} all-reduce(f32[64,64]{0,1:T(8,128)S(1)} %fusion.6), channel_id=1, replica_groups=mesh['dp'=16,'tensor'=8] {'tensor'}, use_global_device_ids=true, to_apply=%region_1.0 | all-reduce | flops 4096 | bytes 32768 | tf_op jit(solution)/shard_map/psum | solution.py:24
  178.5 0.1 copy.7
  178.6 5.8 %cholesky.16 = f32[64,64]{1,0:T(8,128)S(1)} custom-call(f32[64,64]{1,0:T(8,128)S(1)} %fusion.4), custom_call_target="Cholesky" | custom-call | tf_op jit(solution)/shard_map/jit(cholesky)/cholesky | solution.py:8
  184.5 0.6 compare_reduce_fusion
  185.1 0.7 fusion.2
  185.8 4.9 %custom-call.7 = f32[1,64,64]{1,2,0:T(8,128)S(1)} custom-call(f32[1,64,64]{2,1,0:T(8,128)S(1)} %fusion.2), custom_call_target="InvertDiagBlocksLowerTriangular" | custom-call | tf_op jit(solution)/shard_map/jit(_solve_triangular)/triangular_solve | solution.py:9
  190.7 1.6 convolution_convert_fusion
  192.2 6.9 %fusion.7 = f32[2560,64]{1,0:T(8,128)} fusion(bf16[1600,2560]{1,0:T(8,128)(2,1)} %copy-done.1, bf16[1600,64]{0,1:T(8,128)(2,1)S(1)} %convolution_convert_fusion), kind=kOutput, calls=%fused_computation.18 | convolution fusion | flops 524288000 | bytes 9052160 | tf_op jit(solution)/shard_map/dot_general | solution.py:26
  199.1 0.0 all-reduce.5.cloned.1.call-update
  199.1 143.9 %all-reduce.5.cloned.1.call-done = f32[2560,64]{1,0:T(8,128)} async-done(((f32[2560,64]{1,0:T(8,128)}), f32[2560,64]{1,0:T(8,128)}) %all-reduce.5.cloned.1.call-update) | async-done | bytes 655376 | tf_op jit(solution)/shard_map/psum | solution.py:29
  343.0 8.2 %convolution_multiply_fusion = f32[1600,2560]{1,0:T(8,128)S(1)} fusion(bf16[1600,64]{0,1:T(8,128)(2,1)S(1)} %convolution_convert_fusion, f32[2560,64]{1,0:T(8,128)} %all-reduce.5.cloned.1.call-done), kind=kOutput, calls=%fused_computation.3 | convolution fusion | flops 3149824000 | bytes 17244160 | tf_op jit(solution)/shard_map/dot_general | solution.py:30
  351.2 8.0 %fusion.1 = bf16[1,1600,2560]{2,1,0:T(8,128)(2,1)} fusion(f32[1600,2560]{1,0:T(8,128)S(1)} %convolution_multiply_fusion, bf16[1600,2560]{1,0:T(8,128)(2,1)} %copy-done.1), kind=kLoop, calls=%fused_computation.4 | loop fusion | flops 12288000 | bytes 32768000 | tf_op jit(solution)/shard_map/broadcast_in_dim | solution.py:33
  359.2 1.2 dynamic-slice_convert_fusion
  360.4 2.2 copy.8
  (2 shorter events, 0.0 us)
Async XLA Ops:
  7.2 41.8 %copy-start = (bf16[1024,1600]{0,1:T(8,128)(2,1)S(1)}, bf16[1024,1600]{0,1:T(8,128)(2,1)}, u32[]{:S(2)}) copy-start(bf16[1024,1600]{0,1:T(8,128)(2,1)} %param.4) | copy-start | bytes 9830404
  7.2 41.8 %all-gather.2.cloned.1.call-start = ((), (), s32[]{:S(2)}) async-start(), calls=%async_computation | async-start | bytes 5898240 | tf_op jit(solution)/shard_map/all_gather | solution.py:17
  7.9 144.3 %all-reduce.3.cloned.1.call-start = ((), (), s32[]{:S(2)}) async-start(), calls=%async_computation.1 | async-start | bytes 851968 | tf_op jit(solution)/shard_map/psum | solution.py:23
  48.9 15.8 %copy-start.2 = (bf16[2560,64]{0,1:T(8,128)(2,1)S(1)}, bf16[2560,64]{0,1:T(8,128)(2,1)}, u32[]{:S(2)}) copy-start(bf16[2560,64]{0,1:T(8,128)(2,1)} %param.7) | copy-start | bytes 983044
  61.4 3.3 copy-start.1
  68.0 274.9 %all-reduce.5.cloned.1.call-start = ((), (), s32[]{:S(2)}) async-start(), calls=%async_computation.2 | async-start | bytes 2621440 | tf_op jit(solution)/shard_map/psum | solution.py:29
Sparse Core Ops, SparseCore 0:
  9.7 39.1 all-gather.1
  68.2 84.0 all-reduce.2
  199.2 143.7 all-reduce.4
where the time goes:
time: 371 us; the launch traced here: 369 us
  waiting for transfers between devices  270 us (73%)
  matrix products  34.1 us (9%)
  blocking collectives  24.6 us (7%)
  other arithmetic  20.1 us (5%)
  between operations  13.8 us (4%)
  local copies, waits for them, and re-layouts  6.82 us (2%)
    psum x1, waiting for transfers between devices, shards(): q_total = lax.psum(q_term, ('dp', 'tensor'))  144 us
    psum x1, waiting for transfers between devices, shards(): p_total = lax.psum(p_local, 'dp')  84.1 us
    all_gather x1, waiting for transfers between devices, shards(): lax.all_gather(out_grads, 'tensor', axis=0, tiled=True)  41 us
    psum x1, blocking collectives, shards(): lax.psum(jnp.dot(p_total.T, p_total, precision=lax.Precision.HIGHEST), 't...  24.6 us
    dot_general x1, matrix products, shards(): lax.dot_general(hidden_acts, lax.all_gather(out_grads, 'tensor', axis=0,...  12.4 us
    dot_general x1, matrix products, shards(): jnp.dot(p_hat.astype(jnp.float32), q_total.T, precision=lax.Precision.HIG...  8.23 us
    broadcast_in_dim x1, other arithmetic, shards(): new_error = (merged.astype(jnp.float32) - full).astype(jnp.bfloat16)[None]  7.97 us
  transfers between devices with their start and end apart: 3, of which 3 were waited for; matrix products, arithmetic and copies ran while one was open for 0% of the time, Pallas kernels for 0%

commit v1 on v0

v1 whole, which is shorter than its diff:
```python
import functools

import jax
import jax.numpy as jnp
from jax import lax
from jax.experimental import pallas as pl
from jax.experimental.pallas import tpu as pltpu
from jax.sharding import PartitionSpec as P

MESH = pl.DeviceIdType.MESH
F32 = jnp.float32
BF16 = jnp.bfloat16
CHUNK = 256
FILL = {"left_sum": 1, "left_rows": 2, "gram": 2, "right_sum": 3, "right_cross": 2}


def mm(a, b):
    return lax.dot_general(a, b, (((1,), (0,)), ((), ())), preferred_element_type=F32)


def mm_tn(a, b):
    return lax.dot_general(a, b, (((0,), (0,)), ((), ())), preferred_element_type=F32)


def mm_nt(a, b):
    return lax.dot_general(a, b, (((1,), (1,)), ((), ())), preferred_element_type=F32)


def fold(x):
    return x + pltpu.roll(x, x.shape[1] // 2, 1)


def pair(x):
    lane = lax.broadcasted_iota(jnp.int32, x.shape, 1)
    high = x.astype(BF16).astype(F32)
    return jnp.where(lane < x.shape[1] // 2, x, x - high).astype(BF16)


def split_of(n_dp):
    rows = 1
    while rows * rows < n_dp:
        rows *= 2
    return rows, n_dp // rows


def rows_step(total):
    for step in (320, 160, 80, 64, 32, 16):
        if total % step == 0:
            return step
    return total


def step_kernel(
    n_dp, n_t,
    a_hbm, g_hbm, e_hbm, b_hbm,
    merged_hbm, phat_out, qt_out,
    a_ref, at_ref, e_ref, g_own, g_all, basis_ref, bb_ref, merged_ref,
    gb_all, ep_ref, p_send, p_parts, p_all, gram_all, elim_ref,
    pt_ref, y_send, y_parts, q_loc, q_send, q_parts, q_cross,
    load_sem, loc_sem, out_sem, ag_send, ag_recv,
    x1s, x1r, x2s, x2r, x3s, x3r, x4s, x4r, x5s, x5r, x6s, x6r, x7s, x7r, x8s, x8r,
):
    toks, ffl = a_ref.shape
    own_toks, d_model = g_own.shape
    n_chunk = g_all.shape[0]
    width = g_all.shape[2]
    rank = qt_out.shape[0]
    half = own_toks // 2
    part = p_parts.shape[1]
    q_rows, q_cols = q_parts.shape[1:]
    q_split = d_model // q_cols
    d = lax.axis_index("dp")
    t = lax.axis_index("tensor")
    core = lax.rem(t, 2)
    partner = t + 1 - 2 * core
    up = lax.rem(t + 2, n_t)
    down = lax.rem(t + n_t - 2, n_t)
    across = lax.rem(t + 4, n_t)

    def other(block):
        return block + 1 - 2 * lax.rem(block, 2)

    step = rows_step(ffl)
    n_step = ffl // step
    load_g = pltpu.make_async_copy(g_hbm, g_own, load_sem.at[0])
    load_b = pltpu.make_async_copy(b_hbm, basis_ref, load_sem.at[1])
    load_a = pltpu.make_async_copy(a_hbm, a_ref, load_sem.at[2])
    load_g.start()
    load_b.start()

    def load_e(i):
        rows = pl.ds(pl.multiple_of(i * step, step), step)
        return pltpu.make_async_copy(e_hbm.at[0, rows, :], e_ref.at[rows, :], load_sem.at[3 + i])

    for i in range(n_step):
        load_e(i).start()
    load_a.start()

    barrier = pltpu.get_barrier_semaphore()

    def greet_t(k, _):
        pl.semaphore_signal(barrier, inc=1, device_id=(d, lax.rem(t + k, n_t)), device_id_type=MESH)
        return 0

    def greet_d(k, _):
        pl.semaphore_signal(barrier, inc=1, device_id=(lax.rem(d + k, n_dp), t), device_id_type=MESH)
        return 0

    lax.fori_loop(1, n_t, greet_t, 0)
    lax.fori_loop(1, n_dp, greet_d, 0)

    def remote(src, dst, ssem, rsem, dev):
        return pltpu.make_async_remote_copy(
            src_ref=src, dst_ref=dst, send_sem=ssem, recv_sem=rsem, device_id=dev, device_id_type=MESH
        )

    def exchange(n, me, dev, src, dst, ssem, rsem):
        def copy(member, slot):
            return remote(src(member), dst(slot), ssem.at[member], rsem.at[slot], dev(member))

        def loop(body):
            def run(k, _):
                body(lax.rem(me + k, n))
                return 0

            lax.fori_loop(1, n, run, 0)

        return (
            lambda: loop(lambda m: copy(m, me).start()),
            lambda: loop(lambda m: copy(m, m).wait_recv()),
            lambda: loop(lambda m: copy(m, me).wait_send()),
        )

    over_t = functools.partial(exchange, n_t, t, lambda m: (d, m))
    over_dp = functools.partial(exchange, n_dp, d, lambda m: (m, t))

    def block_rows(block):
        return pl.ds(pl.multiple_of(block * own_toks, own_toks), own_toks)

    def top_rows(block):
        return pl.ds(pl.multiple_of(block * own_toks, half), half)

    def low_rows(block):
        return pl.ds(pl.multiple_of(block * own_toks + half, half), half)

    def columns(j):
        return pl.ds(pl.multiple_of(j * width, width), width)

    def own_local(j):
        return pltpu.make_async_copy(g_hbm.at[:, columns(j)], g_all.at[j, block_rows(t), :], loc_sem.at[j])

    def own_to(j, which, dev):
        return remote(
            g_hbm.at[:, columns(j)], g_all.at[j, block_rows(t), :], ag_send.at[j, which], ag_recv.at[j, which], (d, dev)
        )

    def pass_on(j, which, rows, dev):
        ref = g_all.at[j, rows, :]
        return remote(ref, ref, ag_send.at[j, which], ag_recv.at[j, which], (d, dev))

    def start_own(j):
        own_to(j, 0, up).start()
        own_to(j, 1, down).start()
        own_to(j, 2, partner).start()
        own_local(j).start()

    def forward_near(j):
        pass_on(j, 0, block_rows(down), up).wait_recv()
        pass_on(j, 3, top_rows(down), up).start()
        pass_on(j, 5, block_rows(down), partner).start()
        pass_on(j, 1, block_rows(up), down).wait_recv()
        pass_on(j, 4, low_rows(up), down).start()
        pass_on(j, 6, block_rows(up), partner).start()

    def forward_far(j):
        pass_on(j, 3, top_rows(across), up).wait_recv()
        pass_on(j, 4, low_rows(across), down).wait_recv()
        pass_on(j, 7, block_rows(across), partner).start()

    def arrived(j):
        own_local(j).wait()
        pass_on(j, 2, block_rows(partner), partner).wait_recv()
        pass_on(j, 5, block_rows(other(down)), partner).wait_recv()
        pass_on(j, 6, block_rows(other(up)), partner).wait_recv()
        pass_on(j, 7, block_rows(other(across)), partner).wait_recv()

    def merged_out(j):
        return pltpu.make_async_copy(merged_ref.at[:, columns(j)], merged_hbm.at[:, columns(j)], out_sem.at[j])

    def product(j):
        def run(i, _):
            rows = pl.ds(pl.multiple_of(i * step, step), step)
            grad = mm(at_ref[rows, :], g_all[j])
            merged_ref[rows, columns(j)] = (grad + e_ref[rows, columns(j)].astype(F32)).astype(BF16)
            return 0

        lax.fori_loop(0, n_step, run, 0)
        merged_out(j).start()

    ahead = 3

    def chunk(j, _):
        @pl.when(j + ahead < n_chunk)
        def _():
            start_own(j + ahead)

        @pl.when(j + 1 < n_chunk)
        def _():
            forward_near(j + 1)

        forward_far(j)
        arrived(j)
        product(j)
        return 0

    done = 0

    def fill(count):
        nonlocal done
        count = min(count, n_chunk - done)
        if done == 0:
            forward_near(0)
        if count > 0:
            lax.fori_loop(done, done + count, chunk, 0)
        done += count

    load_b.wait()
    bb_ref[...] = jnp.concatenate([basis_ref[...], basis_ref[...]], axis=1)
    load_g.wait()
    gb_all[block_rows(t), :] = pair(mm(g_own[...], bb_ref[...]))
    pl.semaphore_wait(barrier, n_t - 1 + n_dp - 1)
    x1 = over_t(lambda m: gb_all.at[block_rows(t), :], lambda m: gb_all.at[block_rows(m), :], x1s, x1r)
    x1[0]()
    for j in range(min(ahead, n_chunk)):
        start_own(j)

    def error_term(i, _):
        load_e(i).wait()
        rows = pl.ds(pl.multiple_of(i * step, step), step)
        ep_ref[rows, :] = mm(e_ref[rows, :], bb_ref[...])
        return 0

    lax.fori_loop(0, n_step, error_term, 0)
    load_a.wait()
    lanes = 128
    whole = ffl // lanes

    def turn(i, _):
        at = pl.ds(pl.multiple_of(i * lanes, lanes), lanes)
        at_ref[at, :] = a_ref[:, at].T
        return 0

    lax.fori_loop(0, whole, turn, 0)
    if ffl % lanes:
        at_ref[whole * lanes :, :] = a_ref[:, whole * lanes :].T

    x1[1]()

    def left_term(i, _):
        rows = pl.ds(pl.multiple_of(i * step, step), step)
        p_send[rows, :] = pair(fold(mm(at_ref[rows, :], gb_all[...])) + ep_ref[rows, :])
        return 0

    lax.fori_loop(0, n_step, left_term, 0)
    if n_dp * part > ffl:
        p_send[ffl:, :] = jnp.zeros((n_dp * part - ffl, 2 * rank), BF16)

    def part_rows(m):
        return pl.ds(pl.multiple_of(m * part, 16), part)

    x2 = over_dp(lambda m: p_send.at[part_rows(m), :], lambda m: p_parts.at[m], x2s, x2r)
    x2[0]()
    p_parts[d] = p_send[part_rows(d), :]
    fill(FILL["left_sum"])
    x2[1]()
    total = p_parts[0].astype(F32)
    for m in range(1, n_dp):
        total = total + p_parts[m].astype(F32)
    p_all[part_rows(d), :] = pair(fold(total))
    x3 = over_dp(lambda m: p_all.at[part_rows(d), :], lambda m: p_all.at[part_rows(m), :], x3s, x3r)
    x3[0]()
    fill(FILL["left_rows"])
    x3[1]()

    gram = mm_tn(p_all[...], p_all[...])
    gram_all[t] = fold(gram[:rank] + gram[rank:])
    x4 = over_t(lambda m: gram_all.at[t], lambda m: gram_all.at[m], x4s, x4r)
    x4[0]()
    fill(FILL["gram"])
    x4[1]()
    gram = gram_all[0]
    for m in range(1, n_t):
        gram = gram + gram_all[m]

    row_id = lax.broadcasted_iota(jnp.int32, (rank, 2 * rank), 0)
    lane_id = lax.broadcasted_iota(jnp.int32, (rank, 2 * rank), 1)
    elim_ref[...] = jnp.where(lane_id < rank, gram, jnp.where(lane_id - rank == row_id, 1.0, 0.0))

    def eliminate(k, _):
        x = elim_ref[...]
        row = elim_ref[pl.ds(k, 1), :]
        col = jnp.sum(jnp.where(lane_id == k, x, 0.0), axis=1, keepdims=True)
        pivot = jnp.sum(jnp.where(lane_id[:1] == k, row, 0.0), axis=1, keepdims=True)
        factor = jnp.where(row_id > k, col / pivot, 0.0)
        elim_ref[...] = x - factor * row
        return 0

    lax.fori_loop(0, rank, eliminate, 0)
    x = elim_ref[...]
    diag = jnp.sum(jnp.where(lane_id == row_id, x, 0.0), axis=1, keepdims=True)
    x = x * lax.rsqrt(diag)
    inverse = jnp.where(lane_id < rank, pltpu.roll(x, rank, 1), x)
    high = inverse.astype(BF16)
    both = jnp.concatenate([high, (inverse - high.astype(F32)).astype(BF16)], axis=0)

    def hat(i, _):
        rows = pl.ds(pl.multiple_of(i * step, step), step)
        phat_out[rows, :] = fold(mm_nt(p_all[rows, :], both)).astype(BF16)
        return 0

    lax.fori_loop(0, n_step, hat, 0)

    def acts_term(m, _):
        rows = block_rows(m)
        y_send[rows, :] = pair(mm(a_ref[rows, :], phat_out[...]))
        return 0

    lax.fori_loop(0, n_t, acts_term, 0)
    x5 = over_t(lambda m: y_send.at[block_rows(m), :], lambda m: y_parts.at[m], x5s, x5r)
    x5[0]()
    y_parts[t] = y_send[block_rows(t), :]
    pt_ref[...] = phat_out[...].T

    def right_error(j, _):
        q_loc[:, columns(j)] = mm(pt_ref[:rank, :], e_ref[:, columns(j)])
        return 0

    lax.fori_loop(0, n_chunk, right_error, 0)
    x5[1]()
    y = y_parts[0].astype(F32)
    for m in range(1, n_t):
        y = y + y_parts[m].astype(F32)
    y = pair(fold(y))

    def right_term(j, _):
        term = mm_tn(y, g_own[:, columns(j)])
        q_send[:, columns(j)] = (q_loc[:, columns(j)] + term[:rank] + term[rank:]).astype(BF16)
        return 0

    lax.fori_loop(0, n_chunk, right_term, 0)

    def q_block(m):
        return (
            pl.ds(pl.multiple_of(lax.div(m, q_split) * q_rows, 16), q_rows),
            pl.ds(pl.multiple_of(lax.rem(m, q_split) * q_cols, 128), q_cols),
        )

    x6 = over_dp(lambda m: q_send.at[q_block(m)], lambda m: q_parts.at[m], x6s, x6r)
    x6[0]()
    q_parts[d] = q_send[q_block(d)]
    fill(FILL["right_sum"])
    x6[1]()
    q = q_parts[0].astype(F32)
    for m in range(1, n_dp):
        q = q + q_parts[m].astype(F32)
    q_cross[t] = q.astype(BF16)
    x7 = over_t(lambda m: q_cross.at[t], lambda m: q_cross.at[m], x7s, x7r)
    x7[0]()
    fill(FILL["right_cross"])
    x7[1]()
    q = q_cross[0].astype(F32)
    for m in range(1, n_t):
        q = q + q_cross[m].astype(F32)
    qt_out[q_block(d)] = (q / n_dp).astype(BF16)
    x8 = over_dp(lambda m: qt_out.at[q_block(d)], lambda m: qt_out.at[q_block(m)], x8s, x8r)
    x8[0]()
    fill(n_chunk)
    x8[1]()

    for each in (x1, x2, x3, x4, x5, x6, x7, x8):
        each[2]()

    def drain(j, _):
        own_to(j, 0, up).wait_send()
        own_to(j, 1, down).wait_send()
        own_to(j, 2, partner).wait_send()
        pass_on(j, 3, top_rows(down), up).wait_send()
        pass_on(j, 4, low_rows(up), down).wait_send()
        pass_on(j, 5, block_rows(down), partner).wait_send()
        pass_on(j, 6, block_rows(up), partner).wait_send()
        pass_on(j, 7, block_rows(across), partner).wait_send()
        merged_out(j).wait()
        return 0

    lax.fori_loop(0, n_chunk, drain, 0)


def final_kernel(cols, place_ref, merged_ref, phat_ref, qt_ref, update_ref, new_ref, slice_ref):
    rank = qt_ref.shape[0]

    @pl.when(pl.program_id(0) == 0)
    def _():
        moved = pltpu.roll(qt_ref[...].astype(F32), place_ref[0], 1)
        slice_ref[...] = moved[:, :cols].astype(BF16)

    phat = phat_ref[:, :rank]
    full = mm(phat, qt_ref[...])
    new_ref[0] = (merged_ref[...].astype(F32) - full).astype(BF16)
    update_ref[...] = mm(phat, slice_ref[...]).astype(BF16)


def shards(n_dp, n_t, acts, grads, error, basis):
    toks, ffl = acts.shape
    own_toks, d_model = grads.shape
    rank = basis.shape[1]
    width = CHUNK
    n_chunk = d_model // width
    part = -(-ffl // (16 * n_dp)) * 16
    q_split = split_of(n_dp)
    q_rows, q_cols = rank // q_split[0], d_model // q_split[1]
    dma = pltpu.SemaphoreType.DMA
    anywhere = pl.BlockSpec(memory_space=pl.ANY)
    vmem = pl.BlockSpec(memory_space=pltpu.VMEM)
    merged, phat, qt = pl.pallas_call(
        functools.partial(step_kernel, n_dp, n_t),
        out_shape=(
            jax.ShapeDtypeStruct((ffl, d_model), BF16),
            jax.ShapeDtypeStruct((ffl, 2 * rank), BF16),
            jax.ShapeDtypeStruct((rank, d_model), BF16),
        ),
        in_specs=[anywhere] * 4,
        out_specs=(anywhere, vmem, vmem),
        scratch_shapes=[
            pltpu.VMEM((toks, ffl), BF16),
            pltpu.VMEM((ffl, toks), BF16),
            pltpu.VMEM((ffl, d_model), BF16),
            pltpu.VMEM((own_toks, d_model), BF16),
            pltpu.VMEM((n_chunk, toks, width), BF16),
            pltpu.VMEM((d_model, rank), BF16),
            pltpu.VMEM((d_model, 2 * rank), BF16),
            pltpu.VMEM((ffl, d_model), BF16),
            pltpu.VMEM((toks, 2 * rank), BF16),
            pltpu.VMEM((ffl, 2 * rank), F32),
            pltpu.VMEM((n_dp * part, 2 * rank), BF16),
            pltpu.VMEM((n_dp, part, 2 * rank), BF16),
            pltpu.VMEM((n_dp * part, 2 * rank), BF16),
            pltpu.VMEM((n_t, rank, 2 * rank), F32),
            pltpu.VMEM((rank, 2 * rank), F32),
            pltpu.VMEM((2 * rank, ffl), BF16),
            pltpu.VMEM((toks, 2 * rank), BF16),
            pltpu.VMEM((n_t, own_toks, 2 * rank), BF16),
            pltpu.VMEM((rank, d_model), F32),
            pltpu.VMEM((rank, d_model), BF16),
            pltpu.VMEM((n_dp, q_rows, q_cols), BF16),
            pltpu.VMEM((n_t, q_rows, q_cols), BF16),
            dma((3 + ffl // rows_step(ffl),)),
            dma((n_chunk,)),
            dma((n_chunk,)),
            dma((n_chunk, 8)),
            dma((n_chunk, 8)),
        ]
        + [dma((n,)) for n in (n_t, n_dp, n_dp, n_t, n_t, n_dp, n_t, n_dp) for _ in range(2)],
        compiler_params=pltpu.CompilerParams(
            collective_id=0, has_side_effects=True, vmem_limit_bytes=56 * 2**20
        ),
    )(acts, grads, error, basis)

    cols = d_model // n_dp
    step = rows_step(ffl) // 2 if rows_step(ffl) % 32 == 0 else rows_step(ffl)
    place = lax.rem(d_model - lax.axis_index("dp") * cols, d_model).astype(jnp.int32).reshape(1)
    return pl.pallas_call(
        functools.partial(final_kernel, cols),
        grid=(ffl // step,),
        out_shape=(
            jax.ShapeDtypeStruct((ffl, cols), BF16),
            jax.ShapeDtypeStruct((1, ffl, d_model), BF16),
        ),
        in_specs=[
            pl.BlockSpec(memory_space=pltpu.SMEM),
            pl.BlockSpec((step, d_model), lambda i: (i, 0)),
            pl.BlockSpec((step, 2 * rank), lambda i: (i, 0)),
            pl.BlockSpec((rank, d_model), lambda i: (0, 0)),
        ],
        out_specs=(
            pl.BlockSpec((step, cols), lambda i: (i, 0)),
            pl.BlockSpec((1, step, d_model), lambda i: (0, i, 0)),
        ),
        scratch_shapes=[pltpu.VMEM((rank, cols), BF16)],
        compiler_params=pltpu.CompilerParams(vmem_limit_bytes=32 * 2**20),
    )(place, merged, phat, qt)


def solution(mesh):
    n_dp, n_t = mesh.shape["dp"], mesh.shape["tensor"]
    return jax.shard_map(
        functools.partial(shards, n_dp, n_t),
        mesh=mesh,
        in_specs=(P("dp", "tensor"), P(("dp", "tensor"), None), P("dp", "tensor", None), P()),
        out_specs=(P("tensor", "dp"), P("dp", "tensor", None)),
        check_vma=False,
    )
```

time: 371 us -> 113 us (0.30)
  waiting for transfers between devices: 270 us -> 0 us
  Pallas kernels: 0 us -> 96.9 us
  matrix products: 34.1 us -> 0 us
  blocking collectives: 24.6 us -> 0 us
  other arithmetic: 20.1 us -> 0 us
  between operations: 13.8 us -> 0.66 us
  local copies, waits for them, and re-layouts: 6.82 us -> 13.9 us
    psum x2 -> x0, waiting for transfers between devices: 228 us -> none  [the longest x1 144 us: shards(): q_total = lax.psum(q_term, ('dp', 'tensor'))]
    pallas_call x0 -> x2, Pallas kernels: none -> 96.9 us  [the longest x1 90.1 us: shards(): pl.pallas_call(functools.partial(step_kernel, n_dp, n_t), out_shape=(jax....]
    all_gather x1 -> x0, waiting for transfers between devices: 41 us -> none  [shards(): lax.all_gather(out_grads, 'tensor', axis=0, tiled=True)]
    dot_general x5 -> x0, matrix products: 32.5 us -> none  [the longest x1 12.4 us: shards(): lax.dot_general(hidden_acts, lax.all_gather(out_grads, 'tensor', axis=0,...]
    psum x1 -> x0, blocking collectives: 24.6 us -> none  [shards(): lax.psum(jnp.dot(p_total.T, p_total, precision=lax.Precision.HIGHEST), 't...]
    another operation x5 -> x0, other arithmetic: 12.1 us -> none  [the longest x3 6.52 us: orthonormal(): lower = jnp.linalg.cholesky(gram)]
    broadcast_in_dim x1 -> x0, other arithmetic: 7.97 us -> none  [shards(): new_error = (merged.astype(jnp.float32) - full).astype(jnp.bfloat16)[None]]
    unnamed x7 -> x8, local copies, waits for them, and re-layouts: 5.56 us -> 12.8 us
  transfers between devices with their start and end apart: 3 -> 0, of which waited for: 3 -> 0; matrix products, arithmetic and copies ran while one was open for 0% -> 0% of each run, Pallas kernels for 0% -> 0%
where the time goes in v1:
time: 113 us; the launch traced here: 111 us
  Pallas kernels  96.9 us (86%)
  local copies, waits for them, and re-layouts  13.9 us (12%)
    pallas_call x1, Pallas kernels, shards(): pl.pallas_call(functools.partial(step_kernel, n_dp, n_t), out_shape=(jax....  90.1 us
    unnamed x8, local copies, waits for them, and re-layouts  12.8 us
    pallas_call x1, Pallas kernels, shards(): pl.pallas_call(functools.partial(final_kernel, cols), grid=(ffl // step,)...  6.86 us

profile of v1, /device:TPU:0, one launch (start us, length us, event | category | flops | bytes accessed | tf_op | source)
XLA Modules:
  0.0 111.5 jit_solution(13708425295106124274)
XLA Ops:
  0.6 2.1 %copy.7.b_hbm = bf16[2560,64]{1,0:T(8,128)(2,1)} copy(bf16[2560,64]{0,1:T(8,128)(2,1)} %param.7) | data formatting | bytes 655360 | tf_op args[3]
  2.8 5.4 %copy.6.a_hbm = bf16[1024,1600]{1,0:T(8,128)(2,1)} copy(bf16[1024,1600]{0,1:T(8,128)(2,1)} %param.4) | data formatting | bytes 6553600 | tf_op args[0]
  8.2 90.1 %shard_map.59 = (bf16[1600,2560]{1,0:T(8,128)(2,1)}, bf16[1600,128]{1,0:T(8,128)(2,1)}, bf16[64,2560]{1,0:T(8,128)(2,1)}) custom-call(bf16[1024,1600]{1,0:T(8,128)(2,1)} %copy.6.a_hbm, bf16[128,2560]{1,0:T(8,128)(2,1)} %g_hbm.1, bf16[1,1600,2560]{2,1,0:T(8,128)(2,1)} %e_hbm.1, bf16[2560,64]{1,0:T(8,128)(2,1)} %copy.7.b_hbm), custom_call_target="tpu_custom_call" | custom-call | tf_op jit(solution)/shard_map/pallas_call | solution.py:424
  98.2 0.0 copy-start
  98.3 3.3 %copy-done = bf16[1600,2560]{1,0:T(8,128)(2,1)S(1)} copy-done((bf16[1600,2560]{1,0:T(8,128)(2,1)S(1)}, bf16[1600,2560]{1,0:T(8,128)(2,1)}, u32[]{:S(2)}) %copy-start) | copy-done | bytes 8192024
  101.6 0.0 copy-start.1
  101.6 1.0 copy-done.1
  102.6 0.0 copy-start.2
  102.6 1.0 copy-done.2
  103.5 6.9 %shard_map.60 = (bf16[1600,160]{1,0:T(8,128)(2,1)S(1)}, bf16[1,1600,2560]{2,1,0:T(8,128)(2,1)}) custom-call(s32[1]{0:T(128)} %bitcast.place_ref, bf16[1600,2560]{1,0:T(8,128)(2,1)S(1)} %copy-done, bf16[1600,128]{1,0:T(8,128)(2,1)S(1)} %copy-done.1, bf16[64,2560]{1,0:T(8,128)(2,1)S(1)} %copy-done.2), custom_call_target="tpu_custom_call" | custom-call | tf_op jit(solution)/shard_map/pallas_call | solution.py:471
  110.4 1.1 copy.8
Async XLA Ops:
  98.2 3.3 %copy-start = (bf16[1600,2560]{1,0:T(8,128)(2,1)S(1)}, bf16[1600,2560]{1,0:T(8,128)(2,1)}, u32[]{:S(2)}) copy-start(bf16[1600,2560]{1,0:T(8,128)(2,1)} %get-tuple-element.5.merged_ref) | copy-start | bytes 24576004
  101.6 1.0 copy-start.1
  102.6 1.0 copy-start.2

commit v2 on v1

v2 whole, which is shorter than its diff:
```python
import functools

import jax
import jax.numpy as jnp
from jax import lax
from jax.experimental import pallas as pl
from jax.experimental.pallas import tpu as pltpu
from jax.sharding import PartitionSpec as P

MESH = pl.DeviceIdType.MESH
F32 = jnp.float32
BF16 = jnp.bfloat16
CHUNK = 256
WIDE = 512
FILL = {"left_sum": 2, "left_rows": 3, "gram": 0, "right_sum": 2, "right_cross": 2}


def mm(a, b):
    return lax.dot_general(a, b, (((1,), (0,)), ((), ())), preferred_element_type=F32)


def mm_tn(a, b):
    return lax.dot_general(a, b, (((0,), (0,)), ((), ())), preferred_element_type=F32)


def mm_nt(a, b):
    return lax.dot_general(a, b, (((1,), (1,)), ((), ())), preferred_element_type=F32)


def fold(x):
    return x + pltpu.roll(x, x.shape[1] // 2, 1)


def fold_rows(x):
    half = x.shape[0] // 2
    return x[:half] + x[half:]


def pair(x):
    lane = lax.broadcasted_iota(jnp.int32, x.shape, 1)
    high = x.astype(BF16).astype(F32)
    return jnp.where(lane < x.shape[1] // 2, x, x - high).astype(BF16)


def pair_rows(x):
    high = x.astype(BF16)
    return jnp.concatenate([high, (x - high.astype(F32)).astype(BF16)], axis=0)


def split_of(n_dp):
    rows = 1
    while rows * rows < n_dp:
        rows *= 2
    return rows, n_dp // rows


def pieces(total, count):
    while total % (16 * count):
        count -= 1
    return count


def lane_of_diagonal(x, lane_id, row_id):
    return jnp.sum(jnp.where(lane_id == row_id, x, 0.0), axis=1, keepdims=True)


def step_kernel(
    n_dp, n_t,
    at_hbm, g_hbm, e_hbm, bt_hbm,
    merged_ref, phat_out, phat_t_out, qt_out,
    at_ref, e_ref, g_own, g_all, basis_ref, bb_ref,
    gb_all, ep_ref, p_send, p_parts, p_all, pt_ref, gram_all, elim_ref,
    y_send, y_parts, q_loc, q_send, q_parts, q_cross,
    load_sem, e_sem, loc_sem, ag_send, ag_recv,
    x1s, x1r, x2s, x2r, x3s, x3r, x4s, x4r, x5s, x5r, x6s, x6r, x7s, x7r, x8s, x8r,
):
    ffl, toks = at_ref.shape
    own_toks, d_model = g_own.shape
    n_chunk = g_all.shape[0]
    width = g_all.shape[2]
    rank = qt_out.shape[0]
    half = own_toks // 2
    part = p_parts.shape[1]
    q_rows, q_cols = q_parts.shape[1:]
    q_split = d_model // q_cols
    d = lax.axis_index("dp")
    t = lax.axis_index("tensor")
    core = lax.rem(t, 2)
    partner = t + 1 - 2 * core
    up = lax.rem(t + 2, n_t)
    down = lax.rem(t + n_t - 2, n_t)
    across = lax.rem(t + 4, n_t)

    def other(block):
        return block + 1 - 2 * lax.rem(block, 2)

    n_step = e_sem.shape[0]
    step = ffl // n_step
    load_g = pltpu.make_async_copy(g_hbm, g_own, load_sem.at[0])
    load_b = pltpu.make_async_copy(bt_hbm, basis_ref, load_sem.at[1])
    load_a = pltpu.make_async_copy(at_hbm, at_ref, load_sem.at[2])
    load_g.start()
    load_b.start()

    def load_e(i):
        rows = pl.ds(pl.multiple_of(i * step, step), step)
        return pltpu.make_async_copy(e_hbm.at[0, rows, :], e_ref.at[rows, :], e_sem.at[i])

    for i in range(n_step):
        load_e(i).start()
    load_a.start()

    barrier = pltpu.get_barrier_semaphore()

    def greet_t(k, _):
        pl.semaphore_signal(barrier, inc=1, device_id=(d, lax.rem(t + k, n_t)), device_id_type=MESH)
        return 0

    def greet_d(k, _):
        pl.semaphore_signal(barrier, inc=1, device_id=(lax.rem(d + k, n_dp), t), device_id_type=MESH)
        return 0

    lax.fori_loop(1, n_t, greet_t, 0)
    lax.fori_loop(1, n_dp, greet_d, 0)

    def remote(src, dst, ssem, rsem, dev):
        return pltpu.make_async_remote_copy(
            src_ref=src, dst_ref=dst, send_sem=ssem, recv_sem=rsem, device_id=dev, device_id_type=MESH
        )

    def exchange(n, me, dev, src, dst, ssem, rsem):
        def copy(member, slot):
            return remote(src(member), dst(slot), ssem.at[member], rsem.at[slot], dev(member))

        def loop(body):
            def run(k, _):
                body(lax.rem(me + k, n))
                return 0

            lax.fori_loop(1, n, run, 0)

        return (
            lambda: loop(lambda m: copy(m, me).start()),
            lambda: loop(lambda m: copy(m, m).wait_recv()),
            lambda: loop(lambda m: copy(m, me).wait_send()),
        )

    over_t = functools.partial(exchange, n_t, t, lambda m: (d, m))
    over_dp = functools.partial(exchange, n_dp, d, lambda m: (m, t))

    def block_rows(block):
        return pl.ds(pl.multiple_of(block * own_toks, own_toks), own_toks)

    def top_rows(block):
        return pl.ds(pl.multiple_of(block * own_toks, half), half)

    def low_rows(block):
        return pl.ds(pl.multiple_of(block * own_toks + half, half), half)

    def columns(j):
        return pl.ds(pl.multiple_of(j * width, width), width)

    def own_local(j):
        return pltpu.make_async_copy(g_hbm.at[:, columns(j)], g_all.at[j, block_rows(t), :], loc_sem.at[j])

    def own_to(j, which, dev):
        return remote(
            g_hbm.at[:, columns(j)], g_all.at[j, block_rows(t), :], ag_send.at[j, which], ag_recv.at[j, which], (d, dev)
        )

    def pass_on(j, which, rows, dev):
        ref = g_all.at[j, rows, :]
        return remote(ref, ref, ag_send.at[j, which], ag_recv.at[j, which], (d, dev))

    def start_own(j):
        own_to(j, 0, up).start()
        own_to(j, 1, down).start()
        own_to(j, 2, partner).start()
        own_local(j).start()

    def forward_near(j):
        pass_on(j, 0, block_rows(down), up).wait_recv()
        pass_on(j, 3, top_rows(down), up).start()
        pass_on(j, 5, block_rows(down), partner).start()
        pass_on(j, 1, block_rows(up), down).wait_recv()
        pass_on(j, 4, low_rows(up), down).start()
        pass_on(j, 6, block_rows(up), partner).start()

    def forward_far(j):
        pass_on(j, 3, top_rows(across), up).wait_recv()
        pass_on(j, 4, low_rows(across), down).wait_recv()
        pass_on(j, 7, block_rows(across), partner).start()

    def arrived(j):
        own_local(j).wait()
        pass_on(j, 2, block_rows(partner), partner).wait_recv()
        pass_on(j, 5, block_rows(other(down)), partner).wait_recv()
        pass_on(j, 6, block_rows(other(up)), partner).wait_recv()
        pass_on(j, 7, block_rows(other(across)), partner).wait_recv()

    def product(j):
        grad = mm(at_ref[...], g_all[j])
        merged_ref[:, columns(j)] = (grad + e_ref[:, columns(j)].astype(F32)).astype(BF16)

    ahead = 4

    def chunk(j, _):
        @pl.when(j + ahead < n_chunk)
        def _():
            start_own(j + ahead)

        @pl.when(j + 2 < n_chunk)
        def _():
            forward_near(j + 2)

        @pl.when(j + 1 < n_chunk)
        def _():
            forward_far(j + 1)

        arrived(j)
        product(j)
        return 0

    done = 0

    def fill(count):
        nonlocal done
        count = min(count, n_chunk - done)
        if done == 0:
            forward_near(0)
            forward_near(1)
            forward_far(0)
        if count > 0:
            lax.fori_loop(done, done + count, chunk, 0)
        done += count

    load_b.wait()
    bb_ref[...] = jnp.concatenate([basis_ref[...], basis_ref[...]], axis=0).T
    load_g.wait()
    gb_all[block_rows(t), :] = pair(mm(g_own[...], bb_ref[...]))
    pl.semaphore_wait(barrier, n_t - 1 + n_dp - 1)
    x1 = over_t(lambda m: gb_all.at[block_rows(t), :], lambda m: gb_all.at[block_rows(m), :], x1s, x1r)
    x1[0]()
    for j in range(min(ahead, n_chunk)):
        start_own(j)

    def error_term(i, _):
        load_e(i).wait()
        rows = pl.ds(pl.multiple_of(i * step, step), step)
        ep_ref[rows, :] = mm(e_ref[rows, :], bb_ref[...])
        return 0

    lax.fori_loop(0, n_step, error_term, 0)
    load_a.wait()

    x1[1]()

    p_send[:ffl, :] = pair(fold(mm(at_ref[...], gb_all[...])) + ep_ref[...])
    if n_dp * part > ffl:
        p_send[ffl:, :] = jnp.zeros((n_dp * part - ffl, 2 * rank), BF16)

    def part_rows(m):
        return pl.ds(pl.multiple_of(m * part, 16), part)

    x2 = over_dp(lambda m: p_send.at[part_rows(m), :], lambda m: p_parts.at[m], x2s, x2r)
    x2[0]()
    p_parts[d] = p_send[part_rows(d), :]
    fill(FILL["left_sum"])
    x2[1]()
    total = p_parts[0].astype(F32)
    for m in range(1, n_dp):
        total = total + p_parts[m].astype(F32)
    p_all[part_rows(d), :] = pair(fold(total))
    x3 = over_dp(lambda m: p_all.at[part_rows(d), :], lambda m: p_all.at[part_rows(m), :], x3s, x3r)
    x3[0]()
    fill(FILL["left_rows"])
    x3[1]()

    pt_ref[...] = p_all[:ffl, :].T
    gram = fold(fold_rows(mm(pt_ref[...], p_all[:ffl, :])))
    lane_id = lax.broadcasted_iota(jnp.int32, (rank, 2 * rank), 1)
    row_id = lax.broadcasted_iota(jnp.int32, (rank, 2 * rank), 0)
    gram_all[t] = jnp.where(lane_id[: rank // 2] < rank, gram[: rank // 2], gram[rank // 2 :])
    x4 = over_t(lambda m: gram_all.at[t], lambda m: gram_all.at[m], x4s, x4r)
    x4[0]()
    y = pair_rows(fold_rows(mm(pt_ref[...], at_ref[...])))
    for m in range(n_t):
        y_send[m] = y[:, m * own_toks : (m + 1) * own_toks]
    x5 = over_t(lambda m: y_send.at[m], lambda m: y_parts.at[m], x5s, x5r)
    x5[0]()
    y_parts[t] = y_send[t]

    wide = min(WIDE, d_model)

    def wide_columns(j):
        return pl.ds(pl.multiple_of(j * wide, wide), wide)

    def right_error(j, _):
        q_loc[:, wide_columns(j)] = fold_rows(mm(pt_ref[...], e_ref[:, wide_columns(j)]))
        return 0

    lax.fori_loop(0, d_model // wide, right_error, 0)
    fill(FILL["gram"])
    x4[1]()

    gram = gram_all[0]
    for m in range(1, n_t):
        gram = gram + gram_all[m]
    gram = jnp.concatenate([gram, pltpu.roll(gram, rank, 1)], axis=0)
    elim_ref[...] = jnp.where(lane_id < rank, gram, jnp.where(lane_id - rank == row_id, 1.0, 0.0))
    group = 4

    def lane_of(x, k):
        return jnp.sum(jnp.where(lane_id[: x.shape[0]] == k, x, 0.0), axis=1, keepdims=True)

    def eliminate(i, _):
        k = i * group
        x = elim_ref[...]
        rows = [elim_ref[pl.ds(k + a, 1), :] for a in range(group)]
        cols = [lane_of(x, k + a) for a in range(group)]
        corner = [[lane_of(rows[a], k + b) for b in range(group)] for a in range(group)]
        for a in range(group):
            scale = 1.0 / corner[a][a]
            x = x - jnp.where(row_id > k + a, cols[a] * scale, 0.0) * rows[a]
            for b in range(a + 1, group):
                weight = corner[a][b] * scale
                cols[b] = cols[b] - cols[a] * weight
                rows[b] = rows[b] - rows[a] * weight
                for c in range(b, group):
                    corner[b][c] = corner[b][c] - corner[a][c] * weight
        elim_ref[...] = x
        return 0

    lax.fori_loop(0, rank // group, eliminate, 0)
    x = elim_ref[...]
    x = x * lax.rsqrt(lane_of_diagonal(x, lane_id, row_id))
    both = pair_rows(jnp.where(lane_id < rank, pltpu.roll(x, rank, 1), x))

    x5[1]()
    y = y_parts[0].astype(F32)
    for m in range(1, n_t):
        y = y + y_parts[m].astype(F32)
    y = pair_rows(fold_rows(y))

    def right_term(j, _):
        raw = q_loc[:, wide_columns(j)] + fold_rows(mm(y, g_own[:, wide_columns(j)]))
        q_send[:, wide_columns(j)] = fold_rows(mm(both, pair_rows(raw))).astype(BF16)
        return 0

    lax.fori_loop(0, d_model // wide, right_term, 0)

    def q_block(m):
        return (
            pl.ds(pl.multiple_of(lax.div(m, q_split) * q_rows, 16), q_rows),
            pl.ds(pl.multiple_of(lax.rem(m, q_split) * q_cols, 128), q_cols),
        )

    x6 = over_dp(lambda m: q_send.at[q_block(m)], lambda m: q_parts.at[m], x6s, x6r)
    x6[0]()
    q_parts[d] = q_send[q_block(d)]
    phat_out[...] = fold(mm_nt(p_all[:ffl, :], both)).astype(BF16)
    phat_t_out[...] = fold_rows(mm(both, pt_ref[...])).astype(BF16)
    fill(FILL["right_sum"])
    x6[1]()
    q = q_parts[0].astype(F32)
    for m in range(1, n_dp):
        q = q + q_parts[m].astype(F32)
    q_cross[t] = q.astype(BF16)
    x7 = over_t(lambda m: q_cross.at[t], lambda m: q_cross.at[m], x7s, x7r)
    x7[0]()
    fill(FILL["right_cross"])
    x7[1]()
    q = q_cross[0].astype(F32)
    for m in range(1, n_t):
        q = q + q_cross[m].astype(F32)
    qt_out[q_block(d)] = (q / n_dp).astype(BF16)
    x8 = over_dp(lambda m: qt_out.at[q_block(d)], lambda m: qt_out.at[q_block(m)], x8s, x8r)
    x8[0]()
    fill(n_chunk)
    x8[1]()

    for each in (x1, x2, x3, x4, x5, x6, x7, x8):
        each[2]()

    def drain(j, _):
        own_to(j, 0, up).wait_send()
        own_to(j, 1, down).wait_send()
        own_to(j, 2, partner).wait_send()
        pass_on(j, 3, top_rows(down), up).wait_send()
        pass_on(j, 4, low_rows(up), down).wait_send()
        pass_on(j, 5, block_rows(down), partner).wait_send()
        pass_on(j, 6, block_rows(up), partner).wait_send()
        pass_on(j, 7, block_rows(across), partner).wait_send()
        return 0

    lax.fori_loop(0, n_chunk, drain, 0)


def final_kernel(
    merged_ref, phat_ref, phat_t_ref, qt_ref, update_hbm, new_hbm, update_ref, new_ref, update_sem, new_sem
):
    rank, d_model = qt_ref.shape
    cols, ffl = update_ref.shape
    n_step = new_sem.shape[0]
    step = ffl // n_step

    def out(i):
        rows = pl.ds(pl.multiple_of(i * step, step), step)
        return pltpu.make_async_copy(new_ref.at[rows, :], new_hbm.at[0, rows, :], new_sem.at[i])

    def work(i, _):
        rows = pl.ds(pl.multiple_of(i * step, step), step)
        full = mm(phat_ref[rows, :rank], qt_ref[...])
        new_ref[rows, :] = (merged_ref[rows, :].astype(F32) - full).astype(BF16)
        out(i).start()
        return 0

    lax.fori_loop(0, n_step, work, 0)
    shift = lax.rem(d_model - lax.axis_index("dp") * cols, d_model)
    moved = pltpu.roll(qt_ref[...].astype(F32), shift, 1)
    update_ref[...] = mm_tn(moved[:, :cols].astype(BF16), phat_t_ref[...]).astype(BF16)
    update = pltpu.make_async_copy(update_ref, update_hbm, update_sem)
    update.start()

    def ended(i, _):
        out(i).wait()
        return 0

    lax.fori_loop(0, n_step, ended, 0)
    update.wait()


def shards(n_dp, n_t, acts, grads, error, basis):
    ffl, toks = acts.shape[1], acts.shape[0]
    own_toks, d_model = grads.shape
    rank = basis.shape[1]
    width = CHUNK
    n_chunk = d_model // width
    part = -(-ffl // (16 * n_dp)) * 16
    q_split = split_of(n_dp)
    q_rows, q_cols = rank // q_split[0], d_model // q_split[1]
    dma = pltpu.SemaphoreType.DMA
    anywhere = pl.BlockSpec(memory_space=pltpu.HBM)
    vmem = pl.BlockSpec(memory_space=pltpu.VMEM)
    factors = pl.pallas_call(
        functools.partial(step_kernel, n_dp, n_t),
        out_shape=(
            pltpu.VMEM((ffl, d_model), BF16),
            pltpu.VMEM((ffl, 2 * rank), BF16),
            pltpu.VMEM((rank, ffl), BF16),
            pltpu.VMEM((rank, d_model), BF16),
        ),
        in_specs=[anywhere] * 4,
        out_specs=(vmem,) * 4,
        scratch_shapes=[
            pltpu.VMEM((ffl, toks), BF16),
            pltpu.VMEM((ffl, d_model), BF16),
            pltpu.VMEM((own_toks, d_model), BF16),
            pltpu.VMEM((n_chunk, toks, width), BF16),
            pltpu.VMEM((rank, d_model), BF16),
            pltpu.VMEM((d_model, 2 * rank), BF16),
            pltpu.VMEM((toks, 2 * rank), BF16),
            pltpu.VMEM((ffl, 2 * rank), F32),
            pltpu.VMEM((n_dp * part, 2 * rank), BF16),
            pltpu.VMEM((n_dp, part, 2 * rank), BF16),
            pltpu.VMEM((n_dp * part, 2 * rank), BF16),
            pltpu.VMEM((2 * rank, ffl), BF16),
            pltpu.VMEM((n_t, rank // 2, 2 * rank), F32),
            pltpu.VMEM((rank, 2 * rank), F32),
            pltpu.VMEM((n_t, 2 * rank, own_toks), BF16),
            pltpu.VMEM((n_t, 2 * rank, own_toks), BF16),
            pltpu.VMEM((rank, d_model), F32),
            pltpu.VMEM((rank, d_model), BF16),
            pltpu.VMEM((n_dp, q_rows, q_cols), BF16),
            pltpu.VMEM((n_t, q_rows, q_cols), BF16),
            dma((3,)),
            dma((pieces(ffl, 2),)),
            dma((n_chunk,)),
            dma((n_chunk, 8)),
            dma((n_chunk, 8)),
        ]
        + [dma((n,)) for n in (n_t, n_dp, n_dp, n_t, n_t, n_dp, n_t, n_dp) for _ in range(2)],
        compiler_params=pltpu.CompilerParams(
            collective_id=0, has_side_effects=True, vmem_limit_bytes=55 * 2**20
        ),
    )(acts.T, grads, error, basis.T)

    cols = d_model // n_dp
    update, new_error = pl.pallas_call(
        final_kernel,
        out_shape=(
            jax.ShapeDtypeStruct((cols, ffl), BF16),
            jax.ShapeDtypeStruct((1, ffl, d_model), BF16),
        ),
        in_specs=[vmem] * 4,
        out_specs=(anywhere,) * 2,
        scratch_shapes=[
            pltpu.VMEM((cols, ffl), BF16),
            pltpu.VMEM((ffl, d_model), BF16),
            dma,
            dma((pieces(ffl, 5),)),
        ],
        compiler_params=pltpu.CompilerParams(vmem_limit_bytes=40 * 2**20),
    )(*factors)
    return update.T, new_error


def solution(mesh):
    n_dp, n_t = mesh.shape["dp"], mesh.shape["tensor"]
    return jax.shard_map(
        functools.partial(shards, n_dp, n_t),
        mesh=mesh,
        in_specs=(P("dp", "tensor"), P(("dp", "tensor"), None), P("dp", "tensor", None), P()),
        out_specs=(P("tensor", "dp"), P("dp", "tensor", None)),
        check_vma=False,
    )
```

time: 113 us -> 70.8 us (0.63); the launches traced: 111 us -> 70.7 us
  Pallas kernels: 96.9 us -> 70 us
  local copies, waits for them, and re-layouts: 13.9 us -> 0 us
    pallas_call x2, Pallas kernels: 96.9 us -> 70 us  [the longest x1 65.9 us: shards(): pl.pallas_call(functools.partial(step_kernel, n_dp, n_t), out_shape=(pltp...]
    unnamed x8 -> x0, local copies, waits for them, and re-layouts: 12.8 us -> none
where the time goes in v2:
time: 70.8 us; the launch traced here: 70.7 us
  Pallas kernels  70 us (99%)
    pallas_call x1, Pallas kernels, shards(): pl.pallas_call(functools.partial(step_kernel, n_dp, n_t), out_shape=(pltp...  65.9 us
    pallas_call x1, Pallas kernels, shards(): pl.pallas_call(final_kernel, out_shape=(jax.ShapeDtypeStruct((cols, ffl),...  4.16 us

profile of v2, /device:TPU:0, one launch (start us, length us, event | category | flops | bytes accessed | tf_op | source)
XLA Modules:
  0.0 70.7 jit_solution(6274970163810702134)
XLA Ops:
  0.6 65.9 %shard_map.59 = (bf16[1600,2560]{1,0:T(8,128)(2,1)S(1)}, bf16[1600,128]{1,0:T(8,128)(2,1)S(1)}, bf16[64,1600]{1,0:T(8,128)(2,1)S(1)}, bf16[64,2560]{1,0:T(8,128)(2,1)S(1)}) custom-call(bf16[1600,1024]{1,0:T(8,128)(2,1)} %bitcast.3, bf16[128,2560]{1,0:T(8,128)(2,1)} %g_hbm.1, bf16[1,1600,2560]{2,1,0:T(8,128)(2,1)} %e_hbm.1, bf16[64,2560]{1,0:T(8,128)(2,1)} %bitcast.4), custom_call_target="tpu_custom_call" | custom-call | tf_op jit(solution)/shard_map/pallas_call | solution.py:445
  66.5 4.2 %shard_map.60 = (bf16[160,1600]{1,0:T(8,128)(2,1)}, bf16[1,1600,2560]{2,1,0:T(8,128)(2,1)}) custom-call(bf16[1600,2560]{1,0:T(8,128)(2,1)S(1)} %get-tuple-element.8.merged_ref, bf16[1600,128]{1,0:T(8,128)(2,1)S(1)} %get-tuple-element.9.phat_ref, bf16[64,1600]{1,0:T(8,128)(2,1)S(1)} %get-tuple-element.10.phat_t_ref, bf16[64,2560]{1,0:T(8,128)(2,1)S(1)} %get-tuple-element.11.qt_ref), custom_call_target="tpu_custom_call" | custom-call | tf_op jit(solution)/shard_map/pallas_call | solution.py:489

commit v3 on v2

--- a/solution.py
+++ b/solution.py
@@ -12,7 +12,9 @@
 BF16 = jnp.bfloat16
 CHUNK = 256
 WIDE = 512
-FILL = {"left_sum": 2, "left_rows": 3, "gram": 0, "right_sum": 2, "right_cross": 2}
+AHEAD = 4
+SERVE = {"error": 1, "left_sum": 1, "left_rows": 0, "gram": 1, "inverse": 1}
+FILL = {"left_sum": 0, "left_rows": 2, "gram": 0, "right_sum": 3, "right_cross": 2}
 
 
 def mm(a, b):
@@ -94,6 +96,19 @@
     def other(block):
         return block + 1 - 2 * lax.rem(block, 2)
 
+    barrier = pltpu.get_barrier_semaphore()
+
+    def greet_t(k, _):
+        pl.semaphore_signal(barrier, inc=1, device_id=(d, lax.rem(t + k, n_t)), device_id_type=MESH)
+        return 0
+
+    def greet_d(k, _):
+        pl.semaphore_signal(barrier, inc=1, device_id=(lax.rem(d + k, n_dp), t), device_id_type=MESH)
+        return 0
+
+    lax.fori_loop(1, n_t, greet_t, 0)
+    lax.fori_loop(1, n_dp, greet_d, 0)
+
     n_step = e_sem.shape[0]
     step = ffl // n_step
     load_g = pltpu.make_async_copy(g_hbm, g_own, load_sem.at[0])
@@ -110,19 +125,6 @@
         load_e(i).start()
     load_a.start()
 
-    barrier = pltpu.get_barrier_semaphore()
-
-    def greet_t(k, _):
-        pl.semaphore_signal(barrier, inc=1, device_id=(d, lax.rem(t + k, n_t)), device_id_type=MESH)
-        return 0
-
-    def greet_d(k, _):
-        pl.semaphore_signal(barrier, inc=1, device_id=(lax.rem(d + k, n_dp), t), device_id_type=MESH)
-        return 0
-
-    lax.fori_loop(1, n_t, greet_t, 0)
-    lax.fori_loop(1, n_dp, greet_d, 0)
-
     def remote(src, dst, ssem, rsem, dev):
         return pltpu.make_async_remote_copy(
             src_ref=src, dst_ref=dst, send_sem=ssem, recv_sem=rsem, device_id=dev, device_id_type=MESH
@@ -202,47 +204,56 @@
         grad = mm(at_ref[...], g_all[j])
         merged_ref[:, columns(j)] = (grad + e_ref[:, columns(j)].astype(F32)).astype(BF16)
 
-    ahead = 4
-
-    def chunk(j, _):
-        @pl.when(j + ahead < n_chunk)
+    def serve_step(j):
+        @pl.when(j + AHEAD < n_chunk)
         def _():
-            start_own(j + ahead)
-
-        @pl.when(j + 2 < n_chunk)
+            start_own(j + AHEAD)
+
+        @pl.when(j < n_chunk)
         def _():
-            forward_near(j + 2)
-
-        @pl.when(j + 1 < n_chunk)
+            forward_near(j)
+
+        @pl.when(j > 0 and j <= n_chunk if isinstance(j, int) else (j > 0) & (j <= n_chunk))
         def _():
-            forward_far(j + 1)
-
-        arrived(j)
-        product(j)
-        return 0
-
+            forward_far(j - 1)
+
+    served = 0
     done = 0
 
+    def serve(count):
+        nonlocal served
+        count = min(count, n_chunk + 1 - served)
+        for j in range(served, served + count):
+            serve_step(j)
+        served += count
+
     def fill(count):
-        nonlocal done
+        nonlocal served, done
         count = min(count, n_chunk - done)
-        if done == 0:
-            forward_near(0)
-            forward_near(1)
-            forward_far(0)
+        lead = served - done
+
+        def chunk(j, _):
+            serve_step(j + lead)
+            arrived(j)
+            product(j)
+            return 0
+
         if count > 0:
             lax.fori_loop(done, done + count, chunk, 0)
         done += count
+        served = min(served + count, n_chunk + 1)
 
     load_b.wait()
-    bb_ref[...] = jnp.concatenate([basis_ref[...], basis_ref[...]], axis=0).T
+    twice = jnp.concatenate([basis_ref[...], basis_ref[...]], axis=0)
     load_g.wait()
-    gb_all[block_rows(t), :] = pair(mm(g_own[...], bb_ref[...]))
+    gb_all[block_rows(t), :] = pair(mm_nt(g_own[...], twice))
     pl.semaphore_wait(barrier, n_t - 1 + n_dp - 1)
     x1 = over_t(lambda m: gb_all.at[block_rows(t), :], lambda m: gb_all.at[block_rows(m), :], x1s, x1r)
     x1[0]()
-    for j in range(min(ahead, n_chunk)):
+    for j in range(min(AHEAD, n_chunk)):
         start_own(j)
+
+    bb_ref[...] = twice.T
 
     def error_term(i, _):
         load_e(i).wait()
@@ -252,6 +263,7 @@
 
     lax.fori_loop(0, n_step, error_term, 0)
     load_a.wait()
+    serve(SERVE["error"])
 
     x1[1]()
 
@@ -265,6 +277,7 @@
     x2 = over_dp(lambda m: p_send.at[part_rows(m), :], lambda m: p_parts.at[m], x2s, x2r)
     x2[0]()
     p_parts[d] = p_send[part_rows(d), :]
+    serve(SERVE["left_sum"])
     fill(FILL["left_sum"])
     x2[1]()
     total = p_parts[0].astype(F32)
@@ -273,6 +286,7 @@
     p_all[part_rows(d), :] = pair(fold(total))
     x3 = over_dp(lambda m: p_all.at[part_rows(d), :], lambda m: p_all.at[part_rows(m), :], x3s, x3r)
     x3[0]()
+    serve(SERVE["left_rows"])
     fill(FILL["left_rows"])
     x3[1]()
 
@@ -300,6 +314,7 @@
         return 0
 
     lax.fori_loop(0, d_model // wide, right_error, 0)
+    serve(SERVE["gram"])
     fill(FILL["gram"])
     x4[1]()
 
@@ -335,6 +350,8 @@
     x = elim_ref[...]
     x = x * lax.rsqrt(lane_of_diagonal(x, lane_id, row_id))
     both = pair_rows(jnp.where(lane_id < rank, pltpu.roll(x, rank, 1), x))
+
+    serve(SERVE["inverse"])
 
     x5[1]()
     y = y_parts[0].astype(F32)
@@ -377,9 +394,8 @@
     x8 = over_dp(lambda m: qt_out.at[q_block(d)], lambda m: qt_out.at[q_block(m)], x8s, x8r)
     x8[0]()
     fill(n_chunk)
-    x8[1]()
-
-    for each in (x1, x2, x3, x4, x5, x6, x7, x8):
+
+    for each in (x1, x2, x3, x4, x5, x6, x7):
         each[2]()
 
     def drain(j, _):
@@ -394,6 +410,8 @@
         return 0
 
     lax.fori_loop(0, n_chunk, drain, 0)
+    x8[1]()
+    x8[2]()
 
 
 def final_kernel(

time: 70.8 us -> 66.8 us (0.944)
  Pallas kernels: 70 us -> 66 us
    pallas_call x1, Pallas kernels: 65.9 us -> 61.9 us  [shards(): pl.pallas_call(functools.partial(step_kernel, n_dp, n_t), out_shape=(pltp...]
where the time goes in v3:
time: 66.8 us; the launch traced here: 66.7 us
  Pallas kernels  66 us (99%)
    pallas_call x1, Pallas kernels, shards(): pl.pallas_call(functools.partial(step_kernel, n_dp, n_t), out_shape=(pltp...  61.9 us
    pallas_call x1, Pallas kernels, shards(): pl.pallas_call(final_kernel, out_shape=(jax.ShapeDtypeStruct((cols, ffl),...  4.17 us

profile of v3, /device:TPU:0, one launch (start us, length us, event | category | flops | bytes accessed | tf_op | source)
XLA Modules:
  0.0 66.7 jit_solution(9972996710470083143)
XLA Ops:
  0.6 61.9 %shard_map.59 = (bf16[1600,2560]{1,0:T(8,128)(2,1)S(1)}, bf16[1600,128]{1,0:T(8,128)(2,1)S(1)}, bf16[64,1600]{1,0:T(8,128)(2,1)S(1)}, bf16[64,2560]{1,0:T(8,128)(2,1)S(1)}) custom-call(bf16[1600,1024]{1,0:T(8,128)(2,1)} %bitcast.3, bf16[128,2560]{1,0:T(8,128)(2,1)} %g_hbm.1, bf16[1,1600,2560]{2,1,0:T(8,128)(2,1)} %e_hbm.1, bf16[64,2560]{1,0:T(8,128)(2,1)} %bitcast.4), custom_call_target="tpu_custom_call" | custom-call | tf_op jit(solution)/shard_map/pallas_call | solution.py:463
  62.5 4.2 %shard_map.60 = (bf16[160,1600]{1,0:T(8,128)(2,1)}, bf16[1,1600,2560]{2,1,0:T(8,128)(2,1)}) custom-call(bf16[1600,2560]{1,0:T(8,128)(2,1)S(1)} %get-tuple-element.8.merged_ref, bf16[1600,128]{1,0:T(8,128)(2,1)S(1)} %get-tuple-element.9.phat_ref, bf16[64,1600]{1,0:T(8,128)(2,1)S(1)} %get-tuple-element.10.phat_t_ref, bf16[64,2560]{1,0:T(8,128)(2,1)S(1)} %get-tuple-element.11.qt_ref), custom_call_target="tpu_custom_call" | custom-call | tf_op jit(solution)/shard_map/pallas_call | solution.py:507

commit v4 on v3

--- a/solution.py
+++ b/solution.py
@@ -14,7 +14,7 @@
 WIDE = 512
 AHEAD = 4
 SERVE = {"error": 1, "left_sum": 1, "left_rows": 0, "gram": 1, "inverse": 1}
-FILL = {"left_sum": 0, "left_rows": 2, "gram": 0, "right_sum": 3, "right_cross": 2}
+FILL = {"left_sum": 0, "left_rows": 2, "gram": 0, "right_sum": 2, "right_cross": 2}
 
 
 def mm(a, b):
@@ -67,16 +67,17 @@
 
 
 def step_kernel(
-    n_dp, n_t,
+    n_dp, n_t, n_y, n_x,
     at_hbm, g_hbm, e_hbm, bt_hbm,
     merged_ref, phat_out, phat_t_out, qt_out,
     at_ref, e_ref, g_own, g_all, basis_ref, bb_ref,
-    gb_all, ep_ref, p_send, p_parts, p_all, pt_ref, gram_all, elim_ref,
+    gbt_all, gb_all, ep_ref, p_send, p_parts, p_all, pt_ref, gram_all, elim_ref,
     y_send, y_parts, q_loc, q_send, q_parts, q_cross,
     load_sem, e_sem, loc_sem, ag_send, ag_recv,
     x1s, x1r, x2s, x2r, x3s, x3r, x4s, x4r, x5s, x5r, x6s, x6r, x7s, x7r, x8s, x8r,
 ):
-    ffl, toks = at_ref.shape
+    toks = at_ref.shape[1]
+    ffl = merged_ref.shape[0]
     own_toks, d_model = g_own.shape
     n_chunk = g_all.shape[0]
     width = g_all.shape[2]
@@ -84,9 +85,9 @@
     half = own_toks // 2
     part = p_parts.shape[1]
     q_rows, q_cols = q_parts.shape[1:]
-    q_split = d_model // q_cols
     d = lax.axis_index("dp")
     t = lax.axis_index("tensor")
+    y, x = lax.div(d, n_x), lax.rem(d, n_x)
     core = lax.rem(t, 2)
     partner = t + 1 - 2 * core
     up = lax.rem(t + 2, n_t)
@@ -96,6 +97,7 @@
     def other(block):
         return block + 1 - 2 * lax.rem(block, 2)
 
+
     barrier = pltpu.get_barrier_semaphore()
 
     def greet_t(k, _):
@@ -113,7 +115,7 @@
     step = ffl // n_step
     load_g = pltpu.make_async_copy(g_hbm, g_own, load_sem.at[0])
     load_b = pltpu.make_async_copy(bt_hbm, basis_ref, load_sem.at[1])
-    load_a = pltpu.make_async_copy(at_hbm, at_ref, load_sem.at[2])
+    load_a = pltpu.make_async_copy(at_hbm, at_ref.at[:ffl, :], load_sem.at[2])
     load_g.start()
     load_b.start()
 
@@ -130,25 +132,51 @@
             src_ref=src, dst_ref=dst, send_sem=ssem, recv_sem=rsem, device_id=dev, device_id_type=MESH
         )
 
-    def exchange(n, me, dev, src, dst, ssem, rsem):
-        def copy(member, slot):
-            return remote(src(member), dst(slot), ssem.at[member], rsem.at[slot], dev(member))
-
-        def loop(body):
-            def run(k, _):
-                body(lax.rem(me + k, n))
-                return 0
-
-            lax.fori_loop(1, n, run, 0)
-
-        return (
-            lambda: loop(lambda m: copy(m, me).start()),
-            lambda: loop(lambda m: copy(m, m).wait_recv()),
-            lambda: loop(lambda m: copy(m, me).wait_send()),
-        )
-
-    over_t = functools.partial(exchange, n_t, t, lambda m: (d, m))
-    over_dp = functools.partial(exchange, n_dp, d, lambda m: (m, t))
+    def place(dy, dx):
+        return lax.rem(y + dy, n_y) * n_x + lax.rem(x + dx, n_x)
+
+    def hops(dy, dx):
+        return min(dy, n_y - dy) + min(dx, n_x - dx)
+
+    offsets = [(dy, dx) for dy in range(n_y) for dx in range(n_x) if dy or dx]
+    dp_order = [place(*o) for o in sorted(offsets, key=lambda o: hops(*o))]
+    dp_near = sum(hops(*o) < 3 for o in offsets)
+    t_order = [partner, up, down, other(up), other(down), across, other(across)]
+    t_near = 5
+
+    class Exchange:
+        def __init__(self, me, order, near, dev, src, dst, ssem, rsem):
+            self.me, self.order, self.near = me, order, near
+            self.copy = lambda member, slot: remote(src(member), dst(slot), ssem.at[member], rsem.at[slot], dev(member))
+
+        def start_one(self, member):
+            self.copy(member, self.me).start()
+
+        def start(self):
+            for member in self.order:
+                self.start_one(member)
+
+        def received(self, members=None):
+            for member in self.order if members is None else members:
+                self.copy(member, member).wait_recv()
+
+        def sent(self):
+            for member in self.order:
+                self.copy(member, self.me).wait_send()
+
+        def total(self, parts):
+            near, far = self.order[: self.near], self.order[self.near :]
+            self.received(near)
+            value = parts[self.me].astype(F32)
+            for member in near:
+                value = value + parts[member].astype(F32)
+            self.received(far)
+            for member in far:
+                value = value + parts[member].astype(F32)
+            return value
+
+    over_t = functools.partial(Exchange, t, t_order, t_near, lambda m: (d, m))
+    over_dp = functools.partial(Exchange, d, dp_order, dp_near, lambda m: (m, t))
 
     def block_rows(block):
         return pl.ds(pl.multiple_of(block * own_toks, own_toks), own_toks)
@@ -201,7 +229,7 @@
         pass_on(j, 7, block_rows(other(across)), partner).wait_recv()
 
     def product(j):
-        grad = mm(at_ref[...], g_all[j])
+        grad = mm(at_ref[:ffl, :], g_all[j])
         merged_ref[:, columns(j)] = (grad + e_ref[:, columns(j)].astype(F32)).astype(BF16)
 
     def serve_step(j):
@@ -244,16 +272,19 @@
         served = min(served + count, n_chunk + 1)
 
     load_b.wait()
-    twice = jnp.concatenate([basis_ref[...], basis_ref[...]], axis=0)
     load_g.wait()
-    gb_all[block_rows(t), :] = pair(mm_nt(g_own[...], twice))
+    gbt_all[t] = mm_nt(basis_ref[...], g_own[...]).astype(BF16)
     pl.semaphore_wait(barrier, n_t - 1 + n_dp - 1)
-    x1 = over_t(lambda m: gb_all.at[block_rows(t), :], lambda m: gb_all.at[block_rows(m), :], x1s, x1r)
-    x1[0]()
+    x1 = over_t(lambda m: gbt_all.at[t], lambda m: gbt_all.at[m], x1s, x1r)
+    x1.start()
     for j in range(min(AHEAD, n_chunk)):
         start_own(j)
 
-    bb_ref[...] = twice.T
+    bb_ref[...] = jnp.concatenate([basis_ref[...], basis_ref[...]], axis=0).T
+    padded = n_x * n_y * part
+    if padded > ffl:
+        at_ref[ffl:, :] = jnp.zeros((padded - ffl, toks), BF16)
+        ep_ref[ffl:, :] = jnp.zeros((padded - ffl, 2 * rank), F32)
 
     def error_term(i, _):
         load_e(i).wait()
@@ -265,30 +296,29 @@
     load_a.wait()
     serve(SERVE["error"])
 
-    x1[1]()
-
-    p_send[:ffl, :] = pair(fold(mm(at_ref[...], gb_all[...])) + ep_ref[...])
-    if n_dp * part > ffl:
-        p_send[ffl:, :] = jnp.zeros((n_dp * part - ffl, 2 * rank), BF16)
+    x1.received()
+    turned = jnp.concatenate([gbt_all[m] for m in range(n_t)], axis=1)
+    gb_all[...] = jnp.concatenate([turned, turned], axis=0).T
 
     def part_rows(m):
         return pl.ds(pl.multiple_of(m * part, 16), part)
 
     x2 = over_dp(lambda m: p_send.at[part_rows(m), :], lambda m: p_parts.at[m], x2s, x2r)
-    x2[0]()
+    for dy in [*range(1, n_y), 0]:
+        rows = pl.ds(pl.multiple_of(lax.rem(y + dy, n_y) * (n_x * part), 16), n_x * part)
+        p_send[rows, :] = pair(mm(at_ref[rows, :], gb_all[...]) + ep_ref[rows, :])
+        for dx in range(n_x):
+            if dy or dx:
+                x2.start_one(place(dy, dx))
     p_parts[d] = p_send[part_rows(d), :]
     serve(SERVE["left_sum"])
     fill(FILL["left_sum"])
-    x2[1]()
-    total = p_parts[0].astype(F32)
-    for m in range(1, n_dp):
-        total = total + p_parts[m].astype(F32)
-    p_all[part_rows(d), :] = pair(fold(total))
+    p_all[part_rows(d), :] = pair(fold(x2.total(p_parts)))
     x3 = over_dp(lambda m: p_all.at[part_rows(d), :], lambda m: p_all.at[part_rows(m), :], x3s, x3r)
-    x3[0]()
+    x3.start()
     serve(SERVE["left_rows"])
     fill(FILL["left_rows"])
-    x3[1]()
+    x3.received()
 
     pt_ref[...] = p_all[:ffl, :].T
     gram = fold(fold_rows(mm(pt_ref[...], p_all[:ffl, :])))
@@ -296,12 +326,12 @@
     row_id = lax.broadcasted_iota(jnp.int32, (rank, 2 * rank), 0)
     gram_all[t] = jnp.where(lane_id[: rank // 2] < rank, gram[: rank // 2], gram[rank // 2 :])
     x4 = over_t(lambda m: gram_all.at[t], lambda m: gram_all.at[m], x4s, x4r)
-    x4[0]()
-    y = pair_rows(fold_rows(mm(pt_ref[...], at_ref[...])))
+    x4.start()
+    turned = pair_rows(fold_rows(mm(pt_ref[...], at_ref[:ffl, :])))
     for m in range(n_t):
-        y_send[m] = y[:, m * own_toks : (m + 1) * own_toks]
+        y_send[m] = turned[:, m * own_toks : (m + 1) * own_toks]
     x5 = over_t(lambda m: y_send.at[m], lambda m: y_parts.at[m], x5s, x5r)
-    x5[0]()
+    x5.start()
     y_parts[t] = y_send[t]
 
     wide = min(WIDE, d_model)
@@ -316,11 +346,8 @@
     lax.fori_loop(0, d_model // wide, right_error, 0)
     serve(SERVE["gram"])
     fill(FILL["gram"])
-    x4[1]()
-
-    gram = gram_all[0]
-    for m in range(1, n_t):
-        gram = gram + gram_all[m]
+
+    gram = x4.total(gram_all)
     gram = jnp.concatenate([gram, pltpu.roll(gram, rank, 1)], axis=0)
     elim_ref[...] = jnp.where(lane_id < rank, gram, jnp.where(lane_id - rank == row_id, 1.0, 0.0))
     group = 4
@@ -347,56 +374,45 @@
         return 0
 
     lax.fori_loop(0, rank // group, eliminate, 0)
-    x = elim_ref[...]
-    x = x * lax.rsqrt(lane_of_diagonal(x, lane_id, row_id))
-    both = pair_rows(jnp.where(lane_id < rank, pltpu.roll(x, rank, 1), x))
+    reduced = elim_ref[...]
+    reduced = reduced * lax.rsqrt(lane_of_diagonal(reduced, lane_id, row_id))
+    both = pair_rows(jnp.where(lane_id < rank, pltpu.roll(reduced, rank, 1), reduced))
 
     serve(SERVE["inverse"])
 
-    x5[1]()
-    y = y_parts[0].astype(F32)
-    for m in range(1, n_t):
-        y = y + y_parts[m].astype(F32)
-    y = pair_rows(fold_rows(y))
-
-    def right_term(j, _):
-        raw = q_loc[:, wide_columns(j)] + fold_rows(mm(y, g_own[:, wide_columns(j)]))
-        q_send[:, wide_columns(j)] = fold_rows(mm(both, pair_rows(raw))).astype(BF16)
-        return 0
-
-    lax.fori_loop(0, d_model // wide, right_term, 0)
+    acts = pair_rows(fold_rows(x5.total(y_parts)))
 
     def q_block(m):
         return (
-            pl.ds(pl.multiple_of(lax.div(m, q_split) * q_rows, 16), q_rows),
-            pl.ds(pl.multiple_of(lax.rem(m, q_split) * q_cols, 128), q_cols),
+            pl.ds(pl.multiple_of(lax.div(m, n_x) * q_rows, 16), q_rows),
+            pl.ds(pl.multiple_of(lax.rem(m, n_x) * q_cols, 128), q_cols),
         )
 
     x6 = over_dp(lambda m: q_send.at[q_block(m)], lambda m: q_parts.at[m], x6s, x6r)
-    x6[0]()
+    for dx in [*range(1, n_x), 0]:
+        cols = q_block(place(0, dx))[1]
+        raw = q_loc[:, cols] + fold_rows(mm(acts, g_own[:, cols]))
+        q_send[:, cols] = fold_rows(mm(both, pair_rows(raw))).astype(BF16)
+        for dy in range(n_y):
+            if dy or dx:
+                x6.start_one(place(dy, dx))
+
     q_parts[d] = q_send[q_block(d)]
     phat_out[...] = fold(mm_nt(p_all[:ffl, :], both)).astype(BF16)
     phat_t_out[...] = fold_rows(mm(both, pt_ref[...])).astype(BF16)
     fill(FILL["right_sum"])
-    x6[1]()
-    q = q_parts[0].astype(F32)
-    for m in range(1, n_dp):
-        q = q + q_parts[m].astype(F32)
-    q_cross[t] = q.astype(BF16)
+    q_cross[t] = x6.total(q_parts).astype(BF16)
     x7 = over_t(lambda m: q_cross.at[t], lambda m: q_cross.at[m], x7s, x7r)
-    x7[0]()
+    x7.start()
     fill(FILL["right_cross"])
-    x7[1]()
-    q = q_cross[0].astype(F32)
-    for m in range(1, n_t):
-        q = q + q_cross[m].astype(F32)
+    q = x7.total(q_cross)
     qt_out[q_block(d)] = (q / n_dp).astype(BF16)
     x8 = over_dp(lambda m: qt_out.at[q_block(d)], lambda m: qt_out.at[q_block(m)], x8s, x8r)
-    x8[0]()
+    x8.start()
     fill(n_chunk)
 
     for each in (x1, x2, x3, x4, x5, x6, x7):
-        each[2]()
+        each.sent()
 
     def drain(j, _):
         own_to(j, 0, up).wait_send()
@@ -410,8 +426,8 @@
         return 0
 
     lax.fori_loop(0, n_chunk, drain, 0)
-    x8[1]()
-    x8[2]()
+    x8.received()
+    x8.sent()
 
 
 def final_kernel(
@@ -461,7 +477,7 @@
     anywhere = pl.BlockSpec(memory_space=pltpu.HBM)
     vmem = pl.BlockSpec(memory_space=pltpu.VMEM)
     factors = pl.pallas_call(
-        functools.partial(step_kernel, n_dp, n_t),
+        functools.partial(step_kernel, n_dp, n_t, *q_split),
         out_shape=(
             pltpu.VMEM((ffl, d_model), BF16),
             pltpu.VMEM((ffl, 2 * rank), BF16),
@@ -471,14 +487,15 @@
         in_specs=[anywhere] * 4,
         out_specs=(vmem,) * 4,
         scratch_shapes=[
-            pltpu.VMEM((ffl, toks), BF16),
+            pltpu.VMEM((n_dp * part, toks), BF16),
             pltpu.VMEM((ffl, d_model), BF16),
             pltpu.VMEM((own_toks, d_model), BF16),
             pltpu.VMEM((n_chunk, toks, width), BF16),
             pltpu.VMEM((rank, d_model), BF16),
             pltpu.VMEM((d_model, 2 * rank), BF16),
+            pltpu.VMEM((n_t, rank, own_toks), BF16),
             pltpu.VMEM((toks, 2 * rank), BF16),
-            pltpu.VMEM((ffl, 2 * rank), F32),
+            pltpu.VMEM((n_dp * part, 2 * rank), F32),
             pltpu.VMEM((n_dp * part, 2 * rank), BF16),
             pltpu.VMEM((n_dp, part, 2 * rank), BF16),
             pltpu.VMEM((n_dp * part, 2 * rank), BF16),

time: 66.8 us -> 65.5 us (0.981)
  Pallas kernels: 66 us -> 64.8 us
    pallas_call x1, Pallas kernels: 61.9 us -> 60.6 us  [shards(): pl.pallas_call(functools.partial(step_kernel, n_dp, n_t, *q_split), out_s...]
where the time goes in v4:
time: 65.5 us; the launch traced here: 65.4 us
  Pallas kernels  64.8 us (99%)
    pallas_call x1, Pallas kernels, shards(): pl.pallas_call(functools.partial(step_kernel, n_dp, n_t, *q_split), out_s...  60.6 us
    pallas_call x1, Pallas kernels, shards(): pl.pallas_call(final_kernel, out_shape=(jax.ShapeDtypeStruct((cols, ffl),...  4.16 us

profile of v4, /device:TPU:0, one launch (start us, length us, event | category | flops | bytes accessed | tf_op | source)
XLA Modules:
  0.0 65.4 jit_solution(2299637840097151936)
XLA Ops:
  0.6 60.6 %shard_map.59 = (bf16[1600,2560]{1,0:T(8,128)(2,1)S(1)}, bf16[1600,128]{1,0:T(8,128)(2,1)S(1)}, bf16[64,1600]{1,0:T(8,128)(2,1)S(1)}, bf16[64,2560]{1,0:T(8,128)(2,1)S(1)}) custom-call(bf16[1600,1024]{1,0:T(8,128)(2,1)} %bitcast.3, bf16[128,2560]{1,0:T(8,128)(2,1)} %g_hbm.1, bf16[1,1600,2560]{2,1,0:T(8,128)(2,1)} %e_hbm.1, bf16[64,2560]{1,0:T(8,128)(2,1)} %bitcast.4), custom_call_target="tpu_custom_call" | custom-call | tf_op jit(solution)/shard_map/pallas_call | solution.py:479
  61.3 4.2 %shard_map.60 = (bf16[160,1600]{1,0:T(8,128)(2,1)}, bf16[1,1600,2560]{2,1,0:T(8,128)(2,1)}) custom-call(bf16[1600,2560]{1,0:T(8,128)(2,1)S(1)} %get-tuple-element.8.merged_ref, bf16[1600,128]{1,0:T(8,128)(2,1)S(1)} %get-tuple-element.9.phat_ref, bf16[64,1600]{1,0:T(8,128)(2,1)S(1)} %get-tuple-element.10.phat_t_ref, bf16[64,2560]{1,0:T(8,128)(2,1)S(1)} %get-tuple-element.11.qt_ref), custom_call_target="tpu_custom_call" | custom-call | tf_op jit(solution)/shard_map/pallas_call | solution.py:524

commit v5 on v4

--- a/solution.py
+++ b/solution.py
@@ -11,10 +11,10 @@
 F32 = jnp.float32
 BF16 = jnp.bfloat16
 CHUNK = 256
-WIDE = 512
+WIDE = 1280
 AHEAD = 4
 SERVE = {"error": 1, "left_sum": 1, "left_rows": 0, "gram": 1, "inverse": 1}
-FILL = {"left_sum": 0, "left_rows": 2, "gram": 0, "right_sum": 2, "right_cross": 2}
+FILL = {"left_sum": 0, "left_rows": 2, "gram_dp": 0, "gram": 0, "right_sum": 2, "right_cross": 2}
 
 
 def mm(a, b):
@@ -71,10 +71,10 @@
     at_hbm, g_hbm, e_hbm, bt_hbm,
     merged_ref, phat_out, phat_t_out, qt_out,
     at_ref, e_ref, g_own, g_all, basis_ref, bb_ref,
-    gbt_all, gb_all, ep_ref, p_send, p_parts, p_all, pt_ref, gram_all, elim_ref,
+    gbt_all, gb_all, ep_ref, p_send, p_parts, p_all, pt_ref, gram_all, gram_dp, elim_ref,
     y_send, y_parts, q_loc, q_send, q_parts, q_cross,
     load_sem, e_sem, loc_sem, ag_send, ag_recv,
-    x1s, x1r, x2s, x2r, x3s, x3r, x4s, x4r, x5s, x5r, x6s, x6r, x7s, x7r, x8s, x8r,
+    x1s, x1r, x2s, x2r, x3s, x3r, x4s, x4r, x5s, x5r, x6s, x6r, x7s, x7r, x8s, x8r, x9s, x9r,
 ):
     toks = at_ref.shape[1]
     ffl = merged_ref.shape[0]
@@ -145,15 +145,16 @@
     t_near = 5
 
     class Exchange:
-        def __init__(self, me, order, near, dev, src, dst, ssem, rsem):
+        def __init__(self, n, me, order, near, dev, src, dst, ssem, rsem):
             self.me, self.order, self.near = me, order, near
+            self.ring = [lax.rem(me + k, n) for k in range(1, n)]
             self.copy = lambda member, slot: remote(src(member), dst(slot), ssem.at[member], rsem.at[slot], dev(member))
 
         def start_one(self, member):
             self.copy(member, self.me).start()
 
         def start(self):
-            for member in self.order:
+            for member in self.ring:
                 self.start_one(member)
 
         def received(self, members=None):
@@ -175,8 +176,8 @@
                 value = value + parts[member].astype(F32)
             return value
 
-    over_t = functools.partial(Exchange, t, t_order, t_near, lambda m: (d, m))
-    over_dp = functools.partial(Exchange, d, dp_order, dp_near, lambda m: (m, t))
+    over_t = functools.partial(Exchange, n_t, t, t_order, t_near, lambda m: (d, m))
+    over_dp = functools.partial(Exchange, n_dp, d, dp_order, dp_near, lambda m: (m, t))
 
     def block_rows(block):
         return pl.ds(pl.multiple_of(block * own_toks, own_toks), own_toks)
@@ -313,20 +314,26 @@
     p_parts[d] = p_send[part_rows(d), :]
     serve(SERVE["left_sum"])
     fill(FILL["left_sum"])
-    p_all[part_rows(d), :] = pair(fold(x2.total(p_parts)))
+    own = pair(fold(x2.total(p_parts)))
+    p_all[part_rows(d), :] = own
     x3 = over_dp(lambda m: p_all.at[part_rows(d), :], lambda m: p_all.at[part_rows(m), :], x3s, x3r)
     x3.start()
-    serve(SERVE["left_rows"])
-    fill(FILL["left_rows"])
-    x3.received()
-
-    pt_ref[...] = p_all[:ffl, :].T
-    gram = fold(fold_rows(mm(pt_ref[...], p_all[:ffl, :])))
+
+    gram = fold(fold_rows(mm_tn(own, own)))
     lane_id = lax.broadcasted_iota(jnp.int32, (rank, 2 * rank), 1)
     row_id = lax.broadcasted_iota(jnp.int32, (rank, 2 * rank), 0)
     gram_all[t] = jnp.where(lane_id[: rank // 2] < rank, gram[: rank // 2], gram[rank // 2 :])
     x4 = over_t(lambda m: gram_all.at[t], lambda m: gram_all.at[m], x4s, x4r)
     x4.start()
+    serve(SERVE["left_rows"])
+    fill(FILL["left_rows"])
+    gram_dp[d] = x4.total(gram_all)
+    x9 = over_dp(lambda m: gram_dp.at[d], lambda m: gram_dp.at[m], x9s, x9r)
+    x9.start()
+    fill(FILL["gram_dp"])
+    x3.received()
+
+    pt_ref[...] = p_all[:ffl, :].T
     turned = pair_rows(fold_rows(mm(pt_ref[...], at_ref[:ffl, :])))
     for m in range(n_t):
         y_send[m] = turned[:, m * own_toks : (m + 1) * own_toks]
@@ -347,7 +354,7 @@
     serve(SERVE["gram"])
     fill(FILL["gram"])
 
-    gram = x4.total(gram_all)
+    gram = x9.total(gram_dp)
     gram = jnp.concatenate([gram, pltpu.roll(gram, rank, 1)], axis=0)
     elim_ref[...] = jnp.where(lane_id < rank, gram, jnp.where(lane_id - rank == row_id, 1.0, 0.0))
     group = 4
@@ -411,7 +418,7 @@
     x8.start()
     fill(n_chunk)
 
-    for each in (x1, x2, x3, x4, x5, x6, x7):
+    for each in (x1, x2, x3, x4, x5, x6, x7, x9):
         each.sent()
 
     def drain(j, _):
@@ -501,6 +508,7 @@
             pltpu.VMEM((n_dp * part, 2 * rank), BF16),
             pltpu.VMEM((2 * rank, ffl), BF16),
             pltpu.VMEM((n_t, rank // 2, 2 * rank), F32),
+            pltpu.VMEM((n_dp, rank // 2, 2 * rank), F32),
             pltpu.VMEM((rank, 2 * rank), F32),
             pltpu.VMEM((n_t, 2 * rank, own_toks), BF16),
             pltpu.VMEM((n_t, 2 * rank, own_toks), BF16),
@@ -514,7 +522,7 @@
             dma((n_chunk, 8)),
             dma((n_chunk, 8)),
         ]
-        + [dma((n,)) for n in (n_t, n_dp, n_dp, n_t, n_t, n_dp, n_t, n_dp) for _ in range(2)],
+        + [dma((n,)) for n in (n_t, n_dp, n_dp, n_t, n_t, n_dp, n_t, n_dp, n_dp) for _ in range(2)],
         compiler_params=pltpu.CompilerParams(
             collective_id=0, has_side_effects=True, vmem_limit_bytes=55 * 2**20
         ),

time: 65.5 us -> 63.1 us (0.963)
  Pallas kernels: 64.8 us -> 62.4 us
    pallas_call x1, Pallas kernels: 60.6 us -> 58.2 us  [shards(): pl.pallas_call(functools.partial(step_kernel, n_dp, n_t, *q_split), out_s...]
where the time goes in v5:
time: 63.1 us; the launch traced here: 63 us
  Pallas kernels  62.4 us (99%)
  between operations  0.64 us (1%)
    pallas_call x1, Pallas kernels, shards(): pl.pallas_call(functools.partial(step_kernel, n_dp, n_t, *q_split), out_s...  58.2 us
    pallas_call x1, Pallas kernels, shards(): pl.pallas_call(final_kernel, out_shape=(jax.ShapeDtypeStruct((cols, ffl),...  4.17 us

profile of v5, /device:TPU:0, one launch (start us, length us, event | category | flops | bytes accessed | tf_op | source)
XLA Modules:
  0.0 63.0 jit_solution(4969577811340875117)
XLA Ops:
  0.6 58.2 %shard_map.59 = (bf16[1600,2560]{1,0:T(8,128)(2,1)S(1)}, bf16[1600,128]{1,0:T(8,128)(2,1)S(1)}, bf16[64,1600]{1,0:T(8,128)(2,1)S(1)}, bf16[64,2560]{1,0:T(8,128)(2,1)S(1)}) custom-call(bf16[1600,1024]{1,0:T(8,128)(2,1)} %bitcast.3, bf16[128,2560]{1,0:T(8,128)(2,1)} %g_hbm.1, bf16[1,1600,2560]{2,1,0:T(8,128)(2,1)} %e_hbm.1, bf16[64,2560]{1,0:T(8,128)(2,1)} %bitcast.4), custom_call_target="tpu_custom_call" | custom-call | tf_op jit(solution)/shard_map/pallas_call | solution.py:486
  58.9 4.2 %shard_map.60 = (bf16[160,1600]{1,0:T(8,128)(2,1)}, bf16[1,1600,2560]{2,1,0:T(8,128)(2,1)}) custom-call(bf16[1600,2560]{1,0:T(8,128)(2,1)S(1)} %get-tuple-element.8.merged_ref, bf16[1600,128]{1,0:T(8,128)(2,1)S(1)} %get-tuple-element.9.phat_ref, bf16[64,1600]{1,0:T(8,128)(2,1)S(1)} %get-tuple-element.10.phat_t_ref, bf16[64,2560]{1,0:T(8,128)(2,1)S(1)} %get-tuple-element.11.qt_ref), custom_call_target="tpu_custom_call" | custom-call | tf_op jit(solution)/shard_map/pallas_call | solution.py:532

commit v6 on v5

--- a/solution.py
+++ b/solution.py
@@ -412,13 +412,15 @@
     x7 = over_t(lambda m: q_cross.at[t], lambda m: q_cross.at[m], x7s, x7r)
     x7.start()
     fill(FILL["right_cross"])
+    for each in (x1, x2, x3, x4, x5, x9):
+        each.sent()
     q = x7.total(q_cross)
     qt_out[q_block(d)] = (q / n_dp).astype(BF16)
     x8 = over_dp(lambda m: qt_out.at[q_block(d)], lambda m: qt_out.at[q_block(m)], x8s, x8r)
     x8.start()
     fill(n_chunk)
 
-    for each in (x1, x2, x3, x4, x5, x6, x7, x9):
+    for each in (x6, x7):
         each.sent()
 
     def drain(j, _):

time: 63.1 us -> 63.2 us (level)
  no operation moved by 1% of the time
where the time goes in v6:
time: 63.2 us; the launch traced here: 63.1 us
  Pallas kernels  62.4 us (99%)
  between operations  0.64 us (1%)
    pallas_call x1, Pallas kernels, shards(): pl.pallas_call(functools.partial(step_kernel, n_dp, n_t, *q_split), out_s...  58.2 us
    pallas_call x1, Pallas kernels, shards(): pl.pallas_call(final_kernel, out_shape=(jax.ShapeDtypeStruct((cols, ffl),...  4.17 us

profile of v6, /device:TPU:0, one launch (start us, length us, event | category | flops | bytes accessed | tf_op | source)
XLA Modules:
  0.0 63.1 jit_solution(11646223228796279132)
XLA Ops:
  0.6 58.2 %shard_map.59 = (bf16[1600,2560]{1,0:T(8,128)(2,1)S(1)}, bf16[1600,128]{1,0:T(8,128)(2,1)S(1)}, bf16[64,1600]{1,0:T(8,128)(2,1)S(1)}, bf16[64,2560]{1,0:T(8,128)(2,1)S(1)}) custom-call(bf16[1600,1024]{1,0:T(8,128)(2,1)} %bitcast.3, bf16[128,2560]{1,0:T(8,128)(2,1)} %g_hbm.1, bf16[1,1600,2560]{2,1,0:T(8,128)(2,1)} %e_hbm.1, bf16[64,2560]{1,0:T(8,128)(2,1)} %bitcast.4), custom_call_target="tpu_custom_call" | custom-call | tf_op jit(solution)/shard_map/pallas_call | solution.py:488
  58.9 4.2 %shard_map.60 = (bf16[160,1600]{1,0:T(8,128)(2,1)}, bf16[1,1600,2560]{2,1,0:T(8,128)(2,1)}) custom-call(bf16[1600,2560]{1,0:T(8,128)(2,1)S(1)} %get-tuple-element.8.merged_ref, bf16[1600,128]{1,0:T(8,128)(2,1)S(1)} %get-tuple-element.9.phat_ref, bf16[64,1600]{1,0:T(8,128)(2,1)S(1)} %get-tuple-element.10.phat_t_ref, bf16[64,2560]{1,0:T(8,128)(2,1)S(1)} %get-tuple-element.11.qt_ref), custom_call_target="tpu_custom_call" | custom-call | tf_op jit(solution)/shard_map/pallas_call | solution.py:534
